TPU v7x, 32 devices: a whole 2x2x4 slice. The times are simulated.
32 devices in a mesh: section: 8 (over z, core), rows: 4 (over y, x).
Axes of the slice: x: 2, y: 2, z: 4, core: 2. Of those that a mesh axis runs over, the one named last changes fastest.
Arguments:
- activations: bfloat16 [8, 16, 32, 768], P('section', 'rows'), may hold values from -6 to 6
- cotangent: bfloat16 [8, 16, 32, 3072], P('section', None, None, 'rows'), may hold values from -6 to 6
- proj_weight: bfloat16 [768, 3072], P('section', 'rows'), may hold values from -0.21875 to 0.21875
- kernel_taps: bfloat16 [49, 768], replicated, may hold values from -0.875 to 0.875
- ln_gain: float32 [768], replicated, may hold values from 0.1 to 1.9
- ln_shift: float32 [768], replicated, may hold values from -3 to 3
- heights: int32 [8], P('section'), may hold values from 8 to 16, as said below
- widths: int32 [8], P('section'), may hold values from 16 to 32, as said below
Outputs:
- input_grad: bfloat16 [8, 16, 32, 768], P('section', 'rows')
- weight_grad: float32 [768, 3072], P('section', 'rows')
Inputs may be any that keep to these rules, and one draw needn't show every extreme that they name: `heights`: every image has at least half of 16 valid rows, and some image has all 16. `widths`: every image has at least half of 32 valid columns, and some image has all 32.
All inputs are finite; a program needn't handle non-finite values.
Results may differ from a plain program's by a relative error of at most 0.0049.
Values may be sent and summed in bfloat16 or wider, within the bound.
No kernel may reach another device: no remote copies, remote signals or barrier semaphores. Data moves between devices by JAX's collectives and lax.ppermute only.
A program may use at most 64 MiB of HBM per device.

v0:
```python
import functools

import jax
import jax.numpy as jnp
import numpy as np
from jax import lax
from jax.experimental import pallas as pl
from jax.experimental.pallas import tpu as pltpu
from jax.sharding import PartitionSpec as P

epsilon = 1e-06
LANES = 128
VECTOR = 240
SUBLANES = 8


TILE = 4


def cost(operations, moved):
    return pl.CostEstimate(flops=operations, bytes_accessed=moved, transcendentals=0)


def run(kernel, outs, args, scratch=(), estimate=None, aliases=None, name=None):
    held = list(args) + list(outs) + list(scratch)
    taken = sum(int(np.prod(value.shape)) * jnp.dtype(value.dtype).itemsize for value in held)
    vmem = pl.BlockSpec(memory_space=pltpu.VMEM)
    smem = pl.BlockSpec(memory_space=pltpu.SMEM)
    return pl.pallas_call(
        kernel,
        out_shape=tuple(outs),
        in_specs=[smem if arg.dtype == jnp.int32 else vmem for arg in args],
        out_specs=tuple(vmem for _ in outs),
        scratch_shapes=[pltpu.VMEM(value.shape, value.dtype) for value in scratch],
        input_output_aliases=aliases or {},
        compiler_params=pltpu.CompilerParams(vmem_limit_bytes=taken + taken // 8 + (4 << 20)),
        cost_estimate=estimate or cost(1, 1),
        name=name,
    )(*args)


def f32(*shape):
    return jax.ShapeDtypeStruct(shape, jnp.float32)


def bf16(*shape):
    return jax.ShapeDtypeStruct(shape, jnp.bfloat16)


def begin_kernel(out_ref):
    out_ref[...] = jnp.zeros(out_ref.shape, out_ref.dtype)


def prepare_kernel(zero_ref, high_ref, wid_ref, taps_ref, act_ref, wide_ref, valid_ref):
    count, chans = taps_ref.shape
    taps = taps_ref[...].astype(jnp.float32)
    for tap in range(count):
        wide_ref[tap] = jnp.broadcast_to(taps[tap : tap + 1], (SUBLANES, chans))
    _, width, lanes = valid_ref.shape
    columns = lax.broadcasted_iota(jnp.int32, (width, lanes), 0) < wid_ref[0]

    @pl.loop(0, valid_ref.shape[0])
    def _(row):
        valid_ref[row] = jnp.where(columns & (row < high_ref[0]), 1.0, 0.0) + zero_ref[0:1, :]


def prepare(heights, widths, taps, act, height):
    count, chans = taps.shape
    outs = [f32(count, SUBLANES, chans), f32(height, act.shape[1], LANES)]
    estimate = cost(VECTOR * 128 * taps.size, 1)
    zero = run(begin_kernel, [f32(SUBLANES, LANES)], (), estimate=estimate, name="begin")[0]
    args = (zero, heights, widths, taps, act)
    return run(prepare_kernel, outs, args, name="prepare")


def clear_sides(source, width):
    sides = jnp.zeros((source.shape[0], 8, LANES), source.dtype)
    source[:, :8, :] = sides
    source[:, 8 + width :, :] = sides


def conv_rows(load, positions, outs, wide_ref, lanes, width, flip):
    stride = width // SUBLANES
    running = {out: [None] * stride for out in outs}
    for row, position in enumerate(positions):
        users = [out for out in outs if 0 <= position - out <= 6]
        if not users:
            continue
        shifted = [load(row, pl.ds(5 + k, SUBLANES, stride=stride)) for k in range(stride + 6)]
        for out in users:
            for along in range(7):
                tap = (position - out) * 7 + along
                weight = wide_ref[48 - tap if flip else tap, :, lanes]
                for i in range(stride):
                    term = weight * shifted[i + along]
                    before = running[out][i]
                    running[out][i] = term if before is None else before + term
    return running


def forward_kernel(bands, indices, fresh, valid_ref, taps_ref, *refs):
    act_refs, (mixed, source) = refs[: len(indices)], refs[-2:]
    rows_dev, width, _ = act_refs[0].shape
    blocks, height = mixed.shape[0], mixed.shape[1] - 6
    stride = width // SUBLANES
    band = lax.axis_index("rows")
    joined = source.shape[0] // rows_dev
    clear_sides(source, width)
    once = fresh and len(indices) == joined
    firsts = [sender(band, index, bands) * rows_dev for index in indices]

    @pl.loop(0, blocks)
    def _(block):
        lanes = pl.ds(pl.multiple_of(block * LANES, LANES), LANES)
        if fresh:
            mixed[block] = jnp.zeros(mixed.shape[1:], mixed.dtype)
        for start in range(0, len(indices), joined):
            base = firsts[start]
            for first in firsts[start : start + joined]:
                base = jnp.minimum(base, first)
            for first, act_ref in zip(firsts[start:], act_refs[start : start + joined]):
                for i in range(rows_dev):
                    row = first + i
                    value = act_ref[i, :, lanes].astype(jnp.float32) * valid_ref[row]
                    source[row - base, 8 : 8 + width, :] = value
            rows = joined * rows_dev
            for low in range(0, rows + 6, TILE):
                outs = range(low, min(low + TILE, rows + 6))
                positions = [i + 6 for i in range(rows)]
                running = conv_rows(
                    lambda row, columns_of: source[row, columns_of, :],
                    positions, outs, taps_ref, lanes, width, False,
                )
                for out, pieces in running.items():
                    for i, value in enumerate(pieces):
                        columns_of = pl.ds(i, SUBLANES, stride=stride)
                        if not once:
                            value = value + mixed[block, base + out, columns_of, :]
                        mixed[block, base + out, columns_of, :] = value


def forward(valid, wide, acts, indices, bands, before=None):
    rows_dev, width, chans = acts[0].shape
    joined = 2 if bands & (bands - 1) == 0 and len(indices) % 2 == 0 else 1
    extra = () if before is None else (before,)
    return run(
        functools.partial(forward_kernel, bands, indices, before is None),
        [f32(chans // LANES, rows_dev * bands + 6, width, LANES)],
        (valid, wide, *acts, *extra),
        [f32(joined * rows_dev, width + 16, LANES)],
        cost(1, 1) if extra else cost(3 * VECTOR * len(acts) * acts[0].size * 49 * 2, 1),
        {2 + len(acts): 0} if extra else {},
        "forward",
    )[0]


def rows_at_once(height):
    return 2 * TILE if height % (2 * TILE) == 0 else TILE


def normalise_kernel(valid_ref, mixed, gain_ref, shift_ref, normed_ref, centres, spreads):
    blocks, height, width, _ = mixed.shape
    height = height - 6
    chans = blocks * LANES
    many = rows_at_once(height)

    @pl.loop(0, height // many)
    def _(step):
        rows = [step * many + i for i in range(many)]
        sums = [sum(mixed[block, row + 3] for block in range(blocks)) for row in rows]
        for row, value in zip(rows, sums):
            centre = jnp.sum(value, axis=-1, keepdims=True) / chans
            centres[row] = jnp.broadcast_to(centre, (width, LANES))

    @pl.loop(0, height // many)
    def _(step):
        rows = [step * many + i for i in range(many)]
        sums = []
        for row in rows:
            centre = centres[row]
            away = [mixed[block, row + 3] - centre for block in range(blocks)]
            sums.append(sum(value * value for value in away))
        for row, value in zip(rows, sums):
            spread = jnp.sum(value, axis=-1, keepdims=True) / chans
            spreads[row] = jnp.broadcast_to(lax.rsqrt(spread + epsilon), (width, LANES))

    @pl.loop(0, height, unroll=2)
    def _(row):
        rows = pl.ds(pl.multiple_of(row * width, width), width)
        centre, inv = centres[row], spreads[row]
        for block in range(blocks):
            lanes = slice(block * LANES, (block + 1) * LANES)
            unit = (mixed[block, row + 3] - centre) * inv
            value = unit * gain_ref[block : block + 1, :] + shift_ref[block : block + 1, :]
            value = value * valid_ref[row]
            normed_ref[rows, lanes] = value.astype(normed_ref.dtype)


def normalise(valid, mixed, gain, shift):
    blocks, height, width, _ = mixed.shape
    height = height - 6
    outs = [bf16(height * width, blocks * LANES)] + [f32(height, width, LANES)] * 2
    return run(normalise_kernel, outs, (valid, mixed, gain, shift), name="normalise")


def project_kernel(valid_ref, grad_ref, mixed, centres, spreads, gain_ref, *refs):
    mine_ref, other_ref, out_ref, whole, result, means, alongs = refs
    steps, band, _ = mine_ref.shape
    blocks, height, width, _ = mixed.shape
    height = height - 6
    chans = blocks * LANES
    parity, place = parity_and_place()
    for ref, core in ((mine_ref, parity), (other_ref, 1 - parity)):
        for index in range(steps):
            step = sender(place, index, steps)
            start = pl.multiple_of((2 * step + core) * band, 16)
            whole[pl.ds(start, band), :] = ref[index]
    result[...] = lax.dot_general(
        grad_ref[...], whole[...], (((1,), (1,)), ((), ())), preferred_element_type=jnp.float32
    )

    def scaled_unit(row, block):
        rows = pl.ds(pl.multiple_of(row * width, width), width)
        lanes = slice(block * LANES, (block + 1) * LANES)
        scaled = result[rows, lanes] * gain_ref[block : block + 1, :]
        return scaled, (mixed[block, row + 3] - centres[row]) * spreads[row]

    many = rows_at_once(height)

    @pl.loop(0, height // many)
    def _(step):
        sums = []
        for i in range(many):
            row = step * many + i
            pairs = [scaled_unit(row, block) for block in range(blocks)]
            sums.append((row, sum(p[0] for p in pairs), sum(p[0] * p[1] for p in pairs)))
        for row, scaled, product in sums:
            mean = jnp.sum(scaled, axis=-1, keepdims=True) / chans
            means[row] = jnp.broadcast_to(mean, (width, LANES))
            along = jnp.sum(product, axis=-1, keepdims=True) / chans
            alongs[row] = jnp.broadcast_to(along, (width, LANES))

    @pl.loop(0, blocks)
    def _(block):
        clear_sides(out_ref.at[block], width)
        empty = jnp.zeros((3,) + out_ref.shape[2:], out_ref.dtype)
        out_ref[block, :3] = empty
        out_ref[block, 3 + height :] = empty

    @pl.loop(0, height, unroll=2)
    def _(row):
        mean, along = means[row], alongs[row]
        inv = spreads[row] * valid_ref[row]
        for block in range(blocks):
            scaled, unit = scaled_unit(row, block)
            out_ref[block, row + 3, 8 : 8 + width, :] = inv * (scaled - mean - unit * along)


def project(valid, grad, mixed, centres, spreads, gain, mine, other):
    blocks, height, width, _ = mixed.shape
    chans = blocks * LANES
    return run(
        project_kernel,
        [f32(blocks, height, width + 16, LANES)],
        (valid, grad, mixed, centres, spreads, gain, mine, other),
        [bf16(chans, grad.shape[1]), f32(grad.shape[0], chans)] + [f32(*centres.shape)] * 2,
        cost(VECTOR * mixed.size * 12, 8 * mixed.size),
        name="project",
    )[0]


def backward_kernel(index, bands, valid_ref, grad_ref, taps_ref, out_ref, result):
    rows_dev, width, chans = out_ref.shape
    stride = width // SUBLANES
    first = partner(lax.axis_index("rows"), index, bands) * rows_dev

    @pl.loop(0, chans // LANES)
    def _(block):
        lanes = pl.ds(pl.multiple_of(block * LANES, LANES), LANES)
        for low in range(0, rows_dev, TILE):
            outs = range(low, min(low + TILE, rows_dev))
            running = conv_rows(
                lambda row, columns_of: grad_ref[block, first + row, columns_of, :],
                list(range(rows_dev + 6)), outs, taps_ref, lanes, width, True,
            )
            for out, pieces in running.items():
                for i, value in enumerate(pieces):
                    result[out, pl.ds(i, SUBLANES, stride=stride), :] = value
        for row in range(rows_dev):
            out_ref[row, :, lanes] = (result[row] * valid_ref[first + row]).astype(out_ref.dtype)


def backward(valid, grad, taps, index, bands):
    blocks, height, width, _ = grad.shape
    rows_dev, width = (height - 6) // bands, width - 16
    shape = (rows_dev, width, blocks * LANES)
    return run(
        functools.partial(backward_kernel, index, bands),
        [bf16(*shape) if index else f32(*shape)],
        (valid, grad, taps),
        [f32(rows_dev, width, LANES)],
        cost(VECTOR * rows_dev * width * blocks * LANES * 49 * 2, 1),
        name="backward",
    )[0]


def outer_kernel(normed_ref, grad_ref, whole_ref, send_ref):
    pieces, band, hidden = whole_ref.shape
    parity, _ = parity_and_place()
    whole_ref[...] = lax.dot_general(
        normed_ref[...], grad_ref[...], (((0,), (0,)), ((), ())), preferred_element_type=jnp.float32
    ).reshape(pieces, band, hidden)
    for piece in range(pieces // 2):
        send_ref[piece] = whole_ref[2 * piece + 1 - parity].astype(send_ref.dtype)


def outer(normed, grad, count):
    chans, hidden = normed.shape[1], grad.shape[1]
    outs = [f32(count, chans // count, hidden), bf16(count // 2, chans // count, hidden)]
    return run(outer_kernel, outs, (normed, grad), name="outer")


def kept(held_ref, got_ref, level, parity, piece):
    held = held_ref[2 * piece + parity] if level == 1 else held_ref[piece]
    return held + got_ref[piece].astype(jnp.float32)


def fold_kernel(level, held_ref, got_ref, keep_ref, send_ref):
    parity, place = parity_and_place()
    bit = lax.rem(place >> level - 1, 2)
    for piece in range(keep_ref.shape[0]):
        keep_ref[piece] = kept(held_ref, got_ref, level, parity, 2 * piece + bit)
        sent = kept(held_ref, got_ref, level, parity, 2 * piece + 1 - bit)
        send_ref[piece] = sent.astype(send_ref.dtype)


def fold(held, got, level):
    pieces, band, hidden = got.shape
    outs = [f32(pieces // 2, band, hidden), bf16(pieces // 2, band, hidden)]
    return run(functools.partial(fold_kernel, level), outs, (held, got), name="fold")


def finish_kernel(count, parts, *refs):
    back_refs, weight_refs, (back_ref, weight_ref) = refs[:parts], refs[parts:-2], refs[-2:]

    def total(values):
        return sum(ref[...].astype(jnp.float32) for ref in values)

    back_ref[...] = total(back_refs).astype(back_ref.dtype)
    weight_ref[...] = total(weight_refs) / count


def finish(backs, weights, count):
    outs = [bf16(*backs[0].shape), f32(*weights[0].shape)]
    kernel = functools.partial(finish_kernel, count, len(backs))
    return run(kernel, outs, (*backs, *weights), name="finish")


def parity_and_place():
    index = lax.axis_index("section")
    return lax.rem(index, 2), index // 2


def partner(place, index, count):
    return place ^ index if count & (count - 1) == 0 else (place + index) % count


def sender(place, index, count):
    return place ^ index if count & (count - 1) == 0 else (place + count - index) % count


def swap_pairs(value):
    count = lax.axis_size("section")
    return lax.ppermute(value, "section", [(i, i ^ 1) for i in range(count)])


def send_rows(value, index):
    if index == 0:
        return value
    count = lax.axis_size("rows")
    return lax.ppermute(value, "rows", [(i, partner(i, index, count)) for i in range(count)])


def send_section(value, index):
    count = lax.axis_size("section")
    way = [(i, partner(i // 2, index, count // 2) * 2 + i % 2) for i in range(count)]
    return lax.ppermute(value, "section", way)


def stack_kernel(*refs):
    for index, ref in enumerate(refs[:-1]):
        refs[-1][index] = ref[...]


def stack(pieces):
    return run(stack_kernel, [bf16(len(pieces), *pieces[0].shape)], pieces, name="stack")[0]


def send_pieces(block):
    steps = lax.axis_size("section") // 2
    if steps & (steps - 1):
        return {index: send_section(block, index) for index in range(1, steps)}
    return {1 << level: send_section(block, 1 << level) for level in range(steps.bit_length() - 1)}


def gather_pairs(block, sent, first):
    steps = lax.axis_size("section") // 2
    pieces = {0: block}
    for index in sorted(sent, reverse=True):
        if steps & (steps - 1):
            pieces[index] = sent[index]
            continue
        passed = {i ^ index: send_section(after(v, first), index) for i, v in pieces.items() if i}
        pieces = pieces | {index: sent[index]} | passed
    return [pieces[index] for index in range(steps)]


def scatter_section(keep, send):
    count = lax.axis_size("section")
    level, sends = 0, [send]
    while True:
        way = [(i, i ^ 1 << level) for i in range(count)]
        got = lax.ppermute(send, "section", way)
        level += 1
        if got.shape[0] % 2:
            break
        keep, send = fold(keep, got, level)
        sends.append(send)
    rest = keep.shape[0]
    if rest == 1:
        return [keep[0], got[0]], sends
    total = keep + got.astype(jnp.float32)
    place = lax.axis_index("section") >> level
    result = lax.dynamic_index_in_dim(total, place, 0, keepdims=False)
    for shift in range(1, rest):
        piece = lax.dynamic_index_in_dim(total, (place + shift) % rest, 0, keepdims=False)
        way = [(i, (i + (shift << level)) % count) for i in range(count)]
        result = result + lax.ppermute(piece.astype(jnp.bfloat16), "section", way).astype(jnp.float32)
    return [result], sends


def after(value, *others):
    return lax.optimization_barrier((value, others))[0]


def local(activations, cotangent, proj_weight, kernel_taps, ln_gain, ln_shift, heights, widths):
    rows_dev, width_dev, chans = activations.shape[1:]
    height_all = cotangent.shape[1]
    hidden_dev = cotangent.shape[3]
    bands = lax.axis_size("rows")
    count = lax.axis_size("section")
    wide, valid = prepare(heights, widths, kernel_taps, activations[0], height_all)
    gain, shift = (value.reshape(chans // LANES, LANES) for value in (ln_gain, ln_shift))
    grad = cotangent.reshape(-1, hidden_dev)

    acts = [activations[0]] + [send_rows(activations[0], i) for i in range(1, bands)]
    half = bands // 2
    mixed = forward(valid, wide, acts[:half], range(half), bands)
    sent = send_pieces(proj_weight)
    mixed = forward(valid, wide, acts[half:], range(half, bands), bands, mixed)
    proj_mine = stack(gather_pairs(proj_weight, sent, mixed))

    normed, centres, spreads = normalise(after(valid, sent[1]), mixed, gain, shift)
    whole, send = outer(normed, grad, count)
    weights, sends = scatter_section(whole, send)

    proj_other = swap_pairs(proj_mine)
    grads = after(grad, sends[min(1, len(sends) - 1)])
    grad_mixed = project(valid, grads, mixed, centres, spreads, gain, proj_mine, proj_other)
    backs = []
    for i in [*range(2, bands), 1, 0]:
        ready = sends[min(1, len(sends) - 1)] if i > 1 else sends[-1]
        backs.append(send_rows(backward(after(valid, ready), grad_mixed, wide, i, bands), i))
    back, weight_grad = finish(backs, weights, count)
    return (back[None], weight_grad)


def solution(mesh):
    in_specs = (
        P("section", "rows", None, None),
        P("section", None, None, "rows"),
        P("section", "rows"),
        P(),
        P(),
        P(),
        P("section"),
        P("section"),
    )
    out_specs = (P("section", "rows", None, None), P("section", "rows"))
    return jax.shard_map(local, mesh=mesh, in_specs=in_specs, out_specs=out_specs, check_vma=False)
```

profile of v0, /device:TPU:0, one launch (start us, length us, event | category | flops | bytes accessed | tf_op | source)
XLA Modules:
  0.0 43.0 jit_solution(12080870144532478235)
XLA Ops:
  0.7 3.0 %collective-permute-start.3 = (bf16[4,32,768]{2,1,0:T(8,128)(2,1)}, bf16[4,32,768]{2,1,0:T(8,128)(2,1)S(1)}, u32[]{:S(2)}, u32[]{:S(2)}) collective-permute-start(bf16[4,32,768]{2,1,0:T(8,128)(2,1)} %bitcast.10), channel_id=1, source_target_pairs={{0,1},{1,0},{2,3},{3,2},{4,5},{5,4},{6,7},{7,6},{8,9},{9,8},{10,11... | collective-permute-start | bytes 589832 | tf_op jit(solution)/shard_map/ppermute | solution.py:381
  3.7 1.5 %collective-permute-start.1 = (bf16[4,32,768]{2,1,0:T(8,128)(2,1)}, bf16[4,32,768]{2,1,0:T(8,128)(2,1)S(1)}, u32[]{:S(2)}, u32[]{:S(2)}) collective-permute-start(bf16[4,32,768]{2,1,0:T(8,128)(2,1)} %bitcast.11), channel_id=1, source_target_pairs={{0,2},{1,3},{2,0},{3,1},{4,6},{5,7},{6,4},{7,5},{8,10},{9,11},{10,... | collective-permute-start | bytes 589832 | tf_op jit(solution)/shard_map/ppermute | solution.py:381
  5.2 2.0 %collective-permute-start = (bf16[96,768]{1,0:T(8,128)(2,1)}, bf16[96,768]{1,0:T(8,128)(2,1)S(1)}, u32[]{:S(2)}, u32[]{:S(2)}) collective-permute-start(bf16[96,768]{1,0:T(8,128)(2,1)} %refs_0_.1), channel_id=1, source_target_pairs={{0,8},{4,12},{8,0},{12,4},{16,24},{20,28},{24,16},{28,20},{1,9},{5... | collective-permute-start | bytes 442376 | tf_op jit(solution)/shard_map/ppermute | solution.py:387
  7.2 2.6 %collective-permute-start.5 = (bf16[96,768]{1,0:T(8,128)(2,1)}, bf16[96,768]{1,0:T(8,128)(2,1)S(1)}, u32[]{:S(2)}, u32[]{:S(2)}) collective-permute-start(bf16[96,768]{1,0:T(8,128)(2,1)} %refs_0_.1), channel_id=1, source_target_pairs={{0,16},{4,20},{8,24},{12,28},{16,0},{20,4},{24,8},{28,12},{1,17},{... | collective-permute-start | bytes 442376 | tf_op jit(solution)/shard_map/ppermute | solution.py:387
  11.4 2.7 %forward.2.refs_2_ = f32[6,22,32,128]{3,2,1,0:T(8,128)S(1)} custom-call(f32[16,32,128]{2,1,0:T(8,128)S(1)} %get-tuple-element.34.valid_ref, f32[49,8,768]{2,1,0:T(8,128)S(1)} %get-tuple-element.22.taps_ref, bf16[4,32,768]{2,1,0:T(8,128)(2,1)S(1)} %bitcast.14, bf16[4,32,768]{2,1,0:T(8,128)(2,1)S(1)} %collective-permute-done.3.refs_1_), custom_call_target="tpu_custom_call" | custom-call | flops 13872660480 | bytes 1 | tf_op jit(solution)/shard_map/forward/pallas_call | solution.py:29
  14.4 2.7 %forward.3.mixed = f32[6,22,32,128]{3,2,1,0:T(8,128)S(1)} custom-call(f32[16,32,128]{2,1,0:T(8,128)S(1)} %get-tuple-element.34.valid_ref, f32[49,8,768]{2,1,0:T(8,128)S(1)} %get-tuple-element.22.taps_ref, bf16[4,32,768]{2,1,0:T(8,128)(2,1)S(1)} %collective-permute-done.1.refs_0_, ...), custom_call_target="tpu_custom_call", output_to_operand_aliasing={{}: (4, {})} | custom-call | flops 1 | bytes 1 | tf_op jit(solution)/shard_map/forward/pallas_call | solution.py:29
  17.2 1.6 %collective-permute-start.6 = (bf16[96,768]{1,0:T(8,128)(2,1)S(1)}, bf16[96,768]{1,0:T(8,128)(2,1)S(1)}, u32[]{:S(2)}, u32[]{:S(2)}) collective-permute-start(bf16[96,768]{1,0:T(8,128)(2,1)S(1)} %collective-permute-done.5.refs_2_), channel_id=1, source_target_pairs={{0,8},{4,12},{8,0},{12,4},{16,24},{20,28},{24,16},{28,20},{1,9},{5... | collective-permute-start | bytes 442376 | tf_op jit(solution)/shard_map/ppermute | solution.py:387
  18.8 0.9 %normalise.1 = (bf16[512,768]{1,0:T(8,128)(2,1)S(1)}, f32[16,32,128]{2,1,0:T(8,128)S(1)}, f32[16,32,128]{2,1,0:T(8,128)S(1)}) custom-call(f32[16,32,128]{2,1,0:T(8,128)S(1)} %get-tuple-element.34.valid_ref, f32[6,22,32,128]{3,2,1,0:T(8,128)S(1)} %forward.3.mixed, f32[6,128]{1,0:T(8,128)S(1)} %bitcast.16, f32[6,128]{1,0:T(8,128)S(1)} %bitcast.18), custom_call_target="tpu_custom_call" | custom-call | flops 1 | bytes 1 | tf_op jit(solution)/shard_map/normalise/pallas_call | solution.py:29
  19.8 1.0 %outer.1 = (f32[8,96,768]{2,1,0:T(8,128)S(1)}, bf16[4,96,768]{2,1,0:T(8,128)(2,1)S(1)}) custom-call(bf16[512,768]{1,0:T(8,128)(2,1)S(1)} %get-tuple-element.23.normed_ref, bf16[512,768]{1,0:T(8,128)(2,1)S(1)} %bitcast.7), custom_call_target="tpu_custom_call" | custom-call | flops 1 | bytes 1 | tf_op jit(solution)/shard_map/outer/pallas_call | solution.py:29
  20.9 1.5 %collective-permute-done.6.refs_3_ = bf16[96,768]{1,0:T(8,128)(2,1)S(1)} collective-permute-done((bf16[96,768]{1,0:T(8,128)(2,1)S(1)}, bf16[96,768]{1,0:T(8,128)(2,1)S(1)}, u32[]{:S(2)}, u32[]{:S(2)}) %collective-permute-start.6) | collective-permute-done | bytes 147488 | tf_op jit(solution)/shard_map/ppermute | solution.py:387
  23.0 1.3 %collective-permute-start.10 = (bf16[2,96,768]{2,1,0:T(8,128)(2,1)S(1)}, bf16[2,96,768]{2,1,0:T(8,128)(2,1)S(1)}, u32[]{:S(2)}, u32[]{:S(2)}) collective-permute-start(bf16[2,96,768]{2,1,0:T(8,128)(2,1)S(1)} %get-tuple-element.26), channel_id=1, source_target_pairs={{0,8},{4,12},{8,0},{12,4},{16,24},{20,28},{24,16},{28,20},{1,9},{5... | collective-permute-start | bytes 884744 | tf_op jit(solution)/shard_map/ppermute | solution.py:423
  24.5 2.0 %project.1.grad_ref = f32[6,22,48,128]{3,2,1,0:T(8,128)S(1)} custom-call(f32[16,32,128]{2,1,0:T(8,128)S(1)} %get-tuple-element.34.valid_ref, bf16[512,768]{1,0:T(8,128)(2,1)S(1)} %bitcast.8, f32[6,22,32,128]{3,2,1,0:T(8,128)S(1)} %forward.3.mixed, f32[16,32,128]{2,1,0:T(8,128)S(1)} %get-tuple-element.29.centres, ...), custom_call_target="tpu_custom_call" | custom-call | flops 1557135360 | bytes 4325376 | tf_op jit(solution)/shard_map/project/pallas_call | solution.py:29
  26.5 1.3 %backward.5 = bf16[4,32,768]{2,1,0:T(8,128)(2,1)S(1)} custom-call(f32[16,32,128]{2,1,0:T(8,128)S(1)} %get-tuple-element.34.valid_ref, f32[6,22,48,128]{3,2,1,0:T(8,128)S(1)} %project.1.grad_ref, f32[49,8,768]{2,1,0:T(8,128)S(1)} %get-tuple-element.22.taps_ref), custom_call_target="tpu_custom_call" | custom-call | flops 2312110080 | bytes 1 | tf_op jit(solution)/shard_map/backward/pallas_call | solution.py:29
  27.8 2.3 %collective-permute-start.9 = (bf16[4,32,768]{2,1,0:T(8,128)(2,1)S(1)}, bf16[4,32,768]{2,1,0:T(8,128)(2,1)S(1)}, u32[]{:S(2)}, u32[]{:S(2)}) collective-permute-start(bf16[4,32,768]{2,1,0:T(8,128)(2,1)S(1)} %backward.5), channel_id=1, source_target_pairs={{0,3},{1,2},{2,1},{3,0},{4,7},{5,6},{6,5},{7,4},{8,11},{9,10},{10,... | collective-permute-start | bytes 589832 | tf_op jit(solution)/shard_map/ppermute | solution.py:381
  30.1 1.3 %backward.4 = bf16[4,32,768]{2,1,0:T(8,128)(2,1)S(1)} custom-call(f32[16,32,128]{2,1,0:T(8,128)S(1)} %get-tuple-element.34.valid_ref, f32[6,22,48,128]{3,2,1,0:T(8,128)S(1)} %project.1.grad_ref, f32[49,8,768]{2,1,0:T(8,128)S(1)} %get-tuple-element.22.taps_ref), custom_call_target="tpu_custom_call" | custom-call | flops 2312110080 | bytes 1 | tf_op jit(solution)/shard_map/backward/pallas_call | solution.py:29
  31.4 0.6 %collective-permute-start.8 = (bf16[4,32,768]{2,1,0:T(8,128)(2,1)S(1)}, bf16[4,32,768]{2,1,0:T(8,128)(2,1)S(1)}, u32[]{:S(2)}, u32[]{:S(2)}) collective-permute-start(bf16[4,32,768]{2,1,0:T(8,128)(2,1)S(1)} %backward.4), channel_id=1, source_target_pairs={{0,2},{1,3},{2,0},{3,1},{4,6},{5,7},{6,4},{7,5},{8,10},{9,11},{10,... | collective-permute-start | bytes 589832 | tf_op jit(solution)/shard_map/ppermute | solution.py:381
  32.2 2.7 %collective-permute-start.12 = (bf16[1,96,768]{2,1,0:T(8,128)(2,1)S(1)}, bf16[1,96,768]{2,1,0:T(8,128)(2,1)S(1)}, u32[]{:S(2)}, u32[]{:S(2)}) collective-permute-start(bf16[1,96,768]{2,1,0:T(8,128)(2,1)S(1)} %get-tuple-element.33), channel_id=1, source_target_pairs={{0,16},{4,20},{8,24},{12,28},{16,0},{20,4},{24,8},{28,12},{1,17},{... | collective-permute-start | bytes 442376 | tf_op jit(solution)/shard_map/ppermute | solution.py:423
  34.8 1.3 %backward.6 = bf16[4,32,768]{2,1,0:T(8,128)(2,1)S(1)} custom-call(f32[16,32,128]{2,1,0:T(8,128)S(1)} %get-tuple-element.34.valid_ref, f32[6,22,48,128]{3,2,1,0:T(8,128)S(1)} %project.1.grad_ref, f32[49,8,768]{2,1,0:T(8,128)S(1)} %get-tuple-element.22.taps_ref), custom_call_target="tpu_custom_call" | custom-call | flops 2312110080 | bytes 1 | tf_op jit(solution)/shard_map/backward/pallas_call | solution.py:29
  36.1 1.3 %collective-permute-start.11 = (bf16[4,32,768]{2,1,0:T(8,128)(2,1)S(1)}, bf16[4,32,768]{2,1,0:T(8,128)(2,1)S(1)}, u32[]{:S(2)}, u32[]{:S(2)}) collective-permute-start(bf16[4,32,768]{2,1,0:T(8,128)(2,1)S(1)} %backward.6), channel_id=1, source_target_pairs={{0,1},{1,0},{2,3},{3,2},{4,5},{5,4},{6,7},{7,6},{8,9},{9,8},{10,11... | collective-permute-start | bytes 589832 | tf_op jit(solution)/shard_map/ppermute | solution.py:381
  37.5 1.3 %backward.7.refs_3_ = f32[4,32,768]{2,1,0:T(8,128)S(1)} custom-call(f32[16,32,128]{2,1,0:T(8,128)S(1)} %get-tuple-element.34.valid_ref, f32[6,22,48,128]{3,2,1,0:T(8,128)S(1)} %project.1.grad_ref, f32[49,8,768]{2,1,0:T(8,128)S(1)} %get-tuple-element.22.taps_ref), custom_call_target="tpu_custom_call" | custom-call | flops 2312110080 | bytes 1 | tf_op jit(solution)/shard_map/backward/pallas_call | solution.py:29
  38.8 1.2 %collective-permute-done.8.refs_0_ = bf16[4,32,768]{2,1,0:T(8,128)(2,1)S(1)} collective-permute-done((bf16[4,32,768]{2,1,0:T(8,128)(2,1)S(1)}, bf16[4,32,768]{2,1,0:T(8,128)(2,1)S(1)}, u32[]{:S(2)}, u32[]{:S(2)}) %collective-permute-start.8) | collective-permute-done | bytes 196640 | tf_op jit(solution)/shard_map/ppermute | solution.py:381
  39.9 1.5 %collective-permute-done.12 = bf16[1,96,768]{2,1,0:T(8,128)(2,1)S(1)} collective-permute-done((bf16[1,96,768]{2,1,0:T(8,128)(2,1)S(1)}, bf16[1,96,768]{2,1,0:T(8,128)(2,1)S(1)}, u32[]{:S(2)}, u32[]{:S(2)}) %collective-permute-start.12) | collective-permute-done | bytes 147488 | tf_op jit(solution)/shard_map/ppermute | solution.py:423
  41.5 0.7 %collective-permute-done.11.refs_2_ = bf16[4,32,768]{2,1,0:T(8,128)(2,1)S(1)} collective-permute-done((bf16[4,32,768]{2,1,0:T(8,128)(2,1)S(1)}, bf16[4,32,768]{2,1,0:T(8,128)(2,1)S(1)}, u32[]{:S(2)}, u32[]{:S(2)}) %collective-permute-start.11) | collective-permute-done | bytes 196640 | tf_op jit(solution)/shard_map/ppermute | solution.py:381
  42.1 0.9 %finish.1 = (bf16[4,32,768]{2,1,0:T(8,128)(2,1)}, f32[96,768]{1,0:T(8,128)}) custom-call(bf16[4,32,768]{2,1,0:T(8,128)(2,1)S(1)} %collective-permute-done.8.refs_0_, bf16[4,32,768]{2,1,0:T(8,128)(2,1)S(1)} %collective-permute-done.9.refs_1_, bf16[4,32,768]{2,1,0:T(8,128)(2,1)S(1)} %collective-permute-done.11.refs_2_, f32[4,32,768]{2,1,0:T(8,128)S(1)} %backward.7.refs_3_, ...), custom_call_target="tpu_custom_call" | custom-call | flops 1 | bytes 1 | tf_op jit(solution)/shard_map/finish/pallas_call | solution.py:29
  (29 shorter events, 1.6 us)
Async XLA Ops:
  0.6 10.5 %copy-start.1 = (bf16[1,4,32,768]{3,2,1,0:T(8,128)(2,1)S(1)}, bf16[1,4,32,768]{3,2,1,0:T(8,128)(2,1)}, u32[]{:S(2)}) copy-start(bf16[1,4,32,768]{3,2,1,0:T(8,128)(2,1)} %param.8) | copy-start | bytes 589828
  0.6 10.5 %copy-start.3 = (bf16[49,768]{1,0:T(8,128)(2,1)S(1)}, bf16[49,768]{1,0:T(8,128)(2,1)}, u32[]{:S(2)}) copy-start(bf16[49,768]{1,0:T(8,128)(2,1)} %taps_ref.1) | copy-start | bytes 225796
  0.7 10.7 %collective-permute-start.3 = (bf16[4,32,768]{2,1,0:T(8,128)(2,1)}, bf16[4,32,768]{2,1,0:T(8,128)(2,1)S(1)}, u32[]{:S(2)}, u32[]{:S(2)}) collective-permute-start(bf16[4,32,768]{2,1,0:T(8,128)(2,1)} %bitcast.10), channel_id=1, source_target_pairs={{0,1},{1,0},{2,3},{3,2},{4,5},{5,4},{6,7},{7,6},{8,9},{9,8},{10,11... | collective-permute-start | bytes 589832 | tf_op jit(solution)/shard_map/ppermute | solution.py:381
  3.7 10.8 %collective-permute-start.1 = (bf16[4,32,768]{2,1,0:T(8,128)(2,1)}, bf16[4,32,768]{2,1,0:T(8,128)(2,1)S(1)}, u32[]{:S(2)}, u32[]{:S(2)}) collective-permute-start(bf16[4,32,768]{2,1,0:T(8,128)(2,1)} %bitcast.11), channel_id=1, source_target_pairs={{0,2},{1,3},{2,0},{3,1},{4,6},{5,7},{6,4},{7,5},{8,10},{9,11},{10,... | collective-permute-start | bytes 589832 | tf_op jit(solution)/shard_map/ppermute | solution.py:381
  5.2 9.3 %collective-permute-start.2 = (bf16[4,32,768]{2,1,0:T(8,128)(2,1)}, bf16[4,32,768]{2,1,0:T(8,128)(2,1)S(1)}, u32[]{:S(2)}, u32[]{:S(2)}) collective-permute-start(bf16[4,32,768]{2,1,0:T(8,128)(2,1)} %bitcast.12), channel_id=1, source_target_pairs={{0,3},{1,2},{2,1},{3,0},{4,7},{5,6},{6,5},{7,4},{8,11},{9,10},{10,... | collective-permute-start | bytes 589832 | tf_op jit(solution)/shard_map/ppermute | solution.py:381
  5.2 13.6 %collective-permute-start = (bf16[96,768]{1,0:T(8,128)(2,1)}, bf16[96,768]{1,0:T(8,128)(2,1)S(1)}, u32[]{:S(2)}, u32[]{:S(2)}) collective-permute-start(bf16[96,768]{1,0:T(8,128)(2,1)} %refs_0_.1), channel_id=1, source_target_pairs={{0,8},{4,12},{8,0},{12,4},{16,24},{20,28},{24,16},{28,20},{1,9},{5... | collective-permute-start | bytes 442376 | tf_op jit(solution)/shard_map/ppermute | solution.py:387
  7.2 9.9 %collective-permute-start.5 = (bf16[96,768]{1,0:T(8,128)(2,1)}, bf16[96,768]{1,0:T(8,128)(2,1)S(1)}, u32[]{:S(2)}, u32[]{:S(2)}) collective-permute-start(bf16[96,768]{1,0:T(8,128)(2,1)} %refs_0_.1), channel_id=1, source_target_pairs={{0,16},{4,20},{8,24},{12,28},{16,0},{20,4},{24,8},{28,12},{1,17},{... | collective-permute-start | bytes 442376 | tf_op jit(solution)/shard_map/ppermute | solution.py:387
  14.1 4.7 %copy-start.4 = (f32[768]{0:T(1024)S(1)}, f32[768]{0:T(1024)}, u32[]{:S(2)}) copy-start(f32[768]{0:T(1024)} %param.12) | copy-start | bytes 9220
  14.2 4.7 %copy-start.5 = (f32[768]{0:T(1024)S(1)}, f32[768]{0:T(1024)}, u32[]{:S(2)}) copy-start(f32[768]{0:T(1024)} %param.13) | copy-start | bytes 9220
  17.2 2.6 %copy-start = (bf16[1,16,32,768]{3,2,1,0:T(8,128)(2,1)S(1)}, bf16[1,16,32,768]{3,2,1,0:T(8,128)(2,1)}, u32[]{:S(2)}) copy-start(bf16[1,16,32,768]{3,2,1,0:T(8,128)(2,1)} %param.9) | copy-start | bytes 2359300
  17.2 5.2 %copy-start.2 = (bf16[96,768]{1,0:T(8,128)(2,1)S(1)}, bf16[96,768]{1,0:T(8,128)(2,1)}, u32[]{:S(2)}) copy-start(bf16[96,768]{1,0:T(8,128)(2,1)} %refs_0_.1) | copy-start | bytes 442372
  17.2 5.2 %collective-permute-start.6 = (bf16[96,768]{1,0:T(8,128)(2,1)S(1)}, bf16[96,768]{1,0:T(8,128)(2,1)S(1)}, u32[]{:S(2)}, u32[]{:S(2)}) collective-permute-start(bf16[96,768]{1,0:T(8,128)(2,1)S(1)} %collective-permute-done.5.refs_2_), channel_id=1, source_target_pairs={{0,8},{4,12},{8,0},{12,4},{16,24},{20,28},{24,16},{28,20},{1,9},{5... | collective-permute-start | bytes 442376 | tf_op jit(solution)/shard_map/ppermute | solution.py:387
  20.8 2.1 %collective-permute-start.4 = (bf16[4,96,768]{2,1,0:T(8,128)(2,1)S(1)}, bf16[4,96,768]{2,1,0:T(8,128)(2,1)S(1)}, u32[]{:S(2)}, u32[]{:S(2)}) collective-permute-start(bf16[4,96,768]{2,1,0:T(8,128)(2,1)S(1)} %get-tuple-element.25), channel_id=1, source_target_pairs={{0,4},{4,0},{8,12},{12,8},{16,20},{20,16},{24,28},{28,24},{1,5},{5... | collective-permute-start | bytes 1769480 | tf_op jit(solution)/shard_map/ppermute | solution.py:423
  22.4 2.1 %collective-permute-start.7 = (bf16[4,96,768]{2,1,0:T(8,128)(2,1)S(1)}, bf16[4,96,768]{2,1,0:T(8,128)(2,1)S(1)}, u32[]{:S(2)}, u32[]{:S(2)}) collective-permute-start(bf16[4,96,768]{2,1,0:T(8,128)(2,1)S(1)} %stack.1.refs_0_), channel_id=1, source_target_pairs={{0,4},{4,0},{8,12},{12,8},{16,20},{20,16},{24,28},{28,24},{1,5},{5... | collective-permute-start | bytes 1769480 | tf_op jit(solution)/shard_map/ppermute | solution.py:374
  23.0 9.1 %collective-permute-start.10 = (bf16[2,96,768]{2,1,0:T(8,128)(2,1)S(1)}, bf16[2,96,768]{2,1,0:T(8,128)(2,1)S(1)}, u32[]{:S(2)}, u32[]{:S(2)}) collective-permute-start(bf16[2,96,768]{2,1,0:T(8,128)(2,1)S(1)} %get-tuple-element.26), channel_id=1, source_target_pairs={{0,8},{4,12},{8,0},{12,4},{16,24},{20,28},{24,16},{28,20},{1,9},{5... | collective-permute-start | bytes 884744 | tf_op jit(solution)/shard_map/ppermute | solution.py:423
  27.8 11.0 %collective-permute-start.9 = (bf16[4,32,768]{2,1,0:T(8,128)(2,1)S(1)}, bf16[4,32,768]{2,1,0:T(8,128)(2,1)S(1)}, u32[]{:S(2)}, u32[]{:S(2)}) collective-permute-start(bf16[4,32,768]{2,1,0:T(8,128)(2,1)S(1)} %backward.5), channel_id=1, source_target_pairs={{0,3},{1,2},{2,1},{3,0},{4,7},{5,6},{6,5},{7,4},{8,11},{9,10},{10,... | collective-permute-start | bytes 589832 | tf_op jit(solution)/shard_map/ppermute | solution.py:381
  31.4 8.5 %collective-permute-start.8 = (bf16[4,32,768]{2,1,0:T(8,128)(2,1)S(1)}, bf16[4,32,768]{2,1,0:T(8,128)(2,1)S(1)}, u32[]{:S(2)}, u32[]{:S(2)}) collective-permute-start(bf16[4,32,768]{2,1,0:T(8,128)(2,1)S(1)} %backward.4), channel_id=1, source_target_pairs={{0,2},{1,3},{2,0},{3,1},{4,6},{5,7},{6,4},{7,5},{8,10},{9,11},{10,... | collective-permute-start | bytes 589832 | tf_op jit(solution)/shard_map/ppermute | solution.py:381
  32.2 9.3 %collective-permute-start.12 = (bf16[1,96,768]{2,1,0:T(8,128)(2,1)S(1)}, bf16[1,96,768]{2,1,0:T(8,128)(2,1)S(1)}, u32[]{:S(2)}, u32[]{:S(2)}) collective-permute-start(bf16[1,96,768]{2,1,0:T(8,128)(2,1)S(1)} %get-tuple-element.33), channel_id=1, source_target_pairs={{0,16},{4,20},{8,24},{12,28},{16,0},{20,4},{24,8},{28,12},{1,17},{... | collective-permute-start | bytes 442376 | tf_op jit(solution)/shard_map/ppermute | solution.py:423
  36.1 6.0 %collective-permute-start.11 = (bf16[4,32,768]{2,1,0:T(8,128)(2,1)S(1)}, bf16[4,32,768]{2,1,0:T(8,128)(2,1)S(1)}, u32[]{:S(2)}, u32[]{:S(2)}) collective-permute-start(bf16[4,32,768]{2,1,0:T(8,128)(2,1)S(1)} %backward.6), channel_id=1, source_target_pairs={{0,1},{1,0},{2,3},{3,2},{4,5},{5,4},{6,7},{7,6},{8,9},{9,8},{10,11... | collective-permute-start | bytes 589832 | tf_op jit(solution)/shard_map/ppermute | solution.py:381
where the time goes:
time: 43.2 us; the launch traced here: 43 us
  starting transfers between devices  19.1 us (44%)
  Pallas kernels  15.9 us (37%)
  waiting for transfers between devices  5.86 us (14%)
  between operations  2.11 us (5%)
    pallas_call x15, Pallas kernels, run(): pl.pallas_call(kernel, out_shape=tuple(outs), in_specs=[smem if arg.dtype...  15.9 us
    ppermute x6, starting transfers between devices, send_rows(): lax.ppermute(value, 'rows', [(i, partner(i, index, count)) for i in range...  8.7 us
    ppermute x3, starting transfers between devices, send_section(): return lax.ppermute(value, 'section', way)  6.26 us
    ppermute x3, starting transfers between devices, scatter_section(): got = lax.ppermute(send, 'section', way)  4.04 us
    ppermute x6, waiting for transfers between devices, send_rows(): lax.ppermute(value, 'rows', [(i, partner(i, index, count)) for i in range...  2.1 us
    ppermute x3, waiting for transfers between devices, scatter_section(): got = lax.ppermute(send, 'section', way)  2.06 us
    ppermute x3, waiting for transfers between devices, send_section(): return lax.ppermute(value, 'section', way)  1.51 us
  transfers between devices with their start and end apart: 13, of which 8 were waited for; matrix products, arithmetic and copies ran while one was open for 0% of the time, Pallas kernels for 35%

commit v1 on v0

--- a/solution.py
+++ b/solution.py
@@ -15,6 +15,7 @@
 
 
 TILE = 4
+WIDE_TILE = 7
 
 
 def cost(operations, moved):
@@ -124,8 +125,8 @@
                     value = act_ref[i, :, lanes].astype(jnp.float32) * valid_ref[row]
                     source[row - base, 8 : 8 + width, :] = value
             rows = joined * rows_dev
-            for low in range(0, rows + 6, TILE):
-                outs = range(low, min(low + TILE, rows + 6))
+            for low in range(0, rows + 6, WIDE_TILE):
+                outs = range(low, min(low + WIDE_TILE, rows + 6))
                 positions = [i + 6 for i in range(rows)]
                 running = conv_rows(
                     lambda row, columns_of: source[row, columns_of, :],

time: 43.2 us -> 43.3 us (level)
  no operation moved by 1% of the time
where the time goes in v1:
time: 43.3 us; the launch traced here: 43.2 us
  starting transfers between devices  19.2 us (44%)
  Pallas kernels  16.2 us (37%)
  waiting for transfers between devices  5.64 us (13%)
  between operations  2.11 us (5%)
    pallas_call x15, Pallas kernels, run(): pl.pallas_call(kernel, out_shape=tuple(outs), in_specs=[smem if arg.dtype...  16.2 us
    ppermute x6, starting transfers between devices, send_rows(): lax.ppermute(value, 'rows', [(i, partner(i, index, count)) for i in range...  8.81 us
    ppermute x3, starting transfers between devices, send_section(): return lax.ppermute(value, 'section', way)  6.26 us
    ppermute x3, starting transfers between devices, scatter_section(): got = lax.ppermute(send, 'section', way)  4.04 us
    ppermute x3, waiting for transfers between devices, scatter_section(): got = lax.ppermute(send, 'section', way)  2.06 us
    ppermute x6, waiting for transfers between devices, send_rows(): lax.ppermute(value, 'rows', [(i, partner(i, index, count)) for i in range...  1.88 us
    ppermute x3, waiting for transfers between devices, send_section(): return lax.ppermute(value, 'section', way)  1.51 us
  transfers between devices with their start and end apart: 13, of which 8 were waited for; matrix products, arithmetic and copies ran while one was open for 0% of the time, Pallas kernels for 35%

profile of v1, /device:TPU:0, one launch (start us, length us, event | category | flops | bytes accessed | tf_op | source)
XLA Modules:
  0.0 43.2 jit_solution(11938250182754082497)
XLA Ops:
  0.7 3.0 %collective-permute-start.3 = (bf16[4,32,768]{2,1,0:T(8,128)(2,1)}, bf16[4,32,768]{2,1,0:T(8,128)(2,1)S(1)}, u32[]{:S(2)}, u32[]{:S(2)}) collective-permute-start(bf16[4,32,768]{2,1,0:T(8,128)(2,1)} %bitcast.10), channel_id=1, source_target_pairs={{0,1},{1,0},{2,3},{3,2},{4,5},{5,4},{6,7},{7,6},{8,9},{9,8},{10,11... | collective-permute-start | bytes 589832 | tf_op jit(solution)/shard_map/ppermute | solution.py:382
  3.7 1.5 %collective-permute-start.1 = (bf16[4,32,768]{2,1,0:T(8,128)(2,1)}, bf16[4,32,768]{2,1,0:T(8,128)(2,1)S(1)}, u32[]{:S(2)}, u32[]{:S(2)}) collective-permute-start(bf16[4,32,768]{2,1,0:T(8,128)(2,1)} %bitcast.11), channel_id=1, source_target_pairs={{0,2},{1,3},{2,0},{3,1},{4,6},{5,7},{6,4},{7,5},{8,10},{9,11},{10,... | collective-permute-start | bytes 589832 | tf_op jit(solution)/shard_map/ppermute | solution.py:382
  5.2 2.0 %collective-permute-start = (bf16[96,768]{1,0:T(8,128)(2,1)}, bf16[96,768]{1,0:T(8,128)(2,1)S(1)}, u32[]{:S(2)}, u32[]{:S(2)}) collective-permute-start(bf16[96,768]{1,0:T(8,128)(2,1)} %refs_0_.1), channel_id=1, source_target_pairs={{0,8},{4,12},{8,0},{12,4},{16,24},{20,28},{24,16},{28,20},{1,9},{5... | collective-permute-start | bytes 442376 | tf_op jit(solution)/shard_map/ppermute | solution.py:388
  7.2 2.6 %collective-permute-start.5 = (bf16[96,768]{1,0:T(8,128)(2,1)}, bf16[96,768]{1,0:T(8,128)(2,1)S(1)}, u32[]{:S(2)}, u32[]{:S(2)}) collective-permute-start(bf16[96,768]{1,0:T(8,128)(2,1)} %refs_0_.1), channel_id=1, source_target_pairs={{0,16},{4,20},{8,24},{12,28},{16,0},{20,4},{24,8},{28,12},{1,17},{... | collective-permute-start | bytes 442376 | tf_op jit(solution)/shard_map/ppermute | solution.py:388
  11.4 2.8 %forward.2.refs_2_ = f32[6,22,32,128]{3,2,1,0:T(8,128)S(1)} custom-call(f32[16,32,128]{2,1,0:T(8,128)S(1)} %get-tuple-element.34.valid_ref, f32[49,8,768]{2,1,0:T(8,128)S(1)} %get-tuple-element.22.taps_ref, bf16[4,32,768]{2,1,0:T(8,128)(2,1)S(1)} %bitcast.14, bf16[4,32,768]{2,1,0:T(8,128)(2,1)S(1)} %collective-permute-done.3.refs_1_), custom_call_target="tpu_custom_call" | custom-call | flops 13872660480 | bytes 1 | tf_op jit(solution)/shard_map/forward/pallas_call | solution.py:30
  14.4 2.9 %forward.3.mixed = f32[6,22,32,128]{3,2,1,0:T(8,128)S(1)} custom-call(f32[16,32,128]{2,1,0:T(8,128)S(1)} %get-tuple-element.34.valid_ref, f32[49,8,768]{2,1,0:T(8,128)S(1)} %get-tuple-element.22.taps_ref, bf16[4,32,768]{2,1,0:T(8,128)(2,1)S(1)} %collective-permute-done.1.refs_0_, ...), custom_call_target="tpu_custom_call", output_to_operand_aliasing={{}: (4, {})} | custom-call | flops 1 | bytes 1 | tf_op jit(solution)/shard_map/forward/pallas_call | solution.py:30
  17.3 1.6 %collective-permute-start.6 = (bf16[96,768]{1,0:T(8,128)(2,1)S(1)}, bf16[96,768]{1,0:T(8,128)(2,1)S(1)}, u32[]{:S(2)}, u32[]{:S(2)}) collective-permute-start(bf16[96,768]{1,0:T(8,128)(2,1)S(1)} %collective-permute-done.5.refs_2_), channel_id=1, source_target_pairs={{0,8},{4,12},{8,0},{12,4},{16,24},{20,28},{24,16},{28,20},{1,9},{5... | collective-permute-start | bytes 442376 | tf_op jit(solution)/shard_map/ppermute | solution.py:388
  19.0 0.9 %normalise.1 = (bf16[512,768]{1,0:T(8,128)(2,1)S(1)}, f32[16,32,128]{2,1,0:T(8,128)S(1)}, f32[16,32,128]{2,1,0:T(8,128)S(1)}) custom-call(f32[16,32,128]{2,1,0:T(8,128)S(1)} %get-tuple-element.34.valid_ref, f32[6,22,32,128]{3,2,1,0:T(8,128)S(1)} %forward.3.mixed, f32[6,128]{1,0:T(8,128)S(1)} %bitcast.16, f32[6,128]{1,0:T(8,128)S(1)} %bitcast.18), custom_call_target="tpu_custom_call" | custom-call | flops 1 | bytes 1 | tf_op jit(solution)/shard_map/normalise/pallas_call | solution.py:30
  20.0 1.0 %outer.1 = (f32[8,96,768]{2,1,0:T(8,128)S(1)}, bf16[4,96,768]{2,1,0:T(8,128)(2,1)S(1)}) custom-call(bf16[512,768]{1,0:T(8,128)(2,1)S(1)} %get-tuple-element.23.normed_ref, bf16[512,768]{1,0:T(8,128)(2,1)S(1)} %bitcast.7), custom_call_target="tpu_custom_call" | custom-call | flops 1 | bytes 1 | tf_op jit(solution)/shard_map/outer/pallas_call | solution.py:30
  21.0 1.5 %collective-permute-done.6.refs_3_ = bf16[96,768]{1,0:T(8,128)(2,1)S(1)} collective-permute-done((bf16[96,768]{1,0:T(8,128)(2,1)S(1)}, bf16[96,768]{1,0:T(8,128)(2,1)S(1)}, u32[]{:S(2)}, u32[]{:S(2)}) %collective-permute-start.6) | collective-permute-done | bytes 147488 | tf_op jit(solution)/shard_map/ppermute | solution.py:388
  23.2 1.3 %collective-permute-start.10 = (bf16[2,96,768]{2,1,0:T(8,128)(2,1)S(1)}, bf16[2,96,768]{2,1,0:T(8,128)(2,1)S(1)}, u32[]{:S(2)}, u32[]{:S(2)}) collective-permute-start(bf16[2,96,768]{2,1,0:T(8,128)(2,1)S(1)} %get-tuple-element.26), channel_id=1, source_target_pairs={{0,8},{4,12},{8,0},{12,4},{16,24},{20,28},{24,16},{28,20},{1,9},{5... | collective-permute-start | bytes 884744 | tf_op jit(solution)/shard_map/ppermute | solution.py:424
  24.7 2.0 %project.1.grad_ref = f32[6,22,48,128]{3,2,1,0:T(8,128)S(1)} custom-call(f32[16,32,128]{2,1,0:T(8,128)S(1)} %get-tuple-element.34.valid_ref, bf16[512,768]{1,0:T(8,128)(2,1)S(1)} %bitcast.8, f32[6,22,32,128]{3,2,1,0:T(8,128)S(1)} %forward.3.mixed, f32[16,32,128]{2,1,0:T(8,128)S(1)} %get-tuple-element.29.centres, ...), custom_call_target="tpu_custom_call" | custom-call | flops 1557135360 | bytes 4325376 | tf_op jit(solution)/shard_map/project/pallas_call | solution.py:30
  26.6 1.3 %backward.5 = bf16[4,32,768]{2,1,0:T(8,128)(2,1)S(1)} custom-call(f32[16,32,128]{2,1,0:T(8,128)S(1)} %get-tuple-element.34.valid_ref, f32[6,22,48,128]{3,2,1,0:T(8,128)S(1)} %project.1.grad_ref, f32[49,8,768]{2,1,0:T(8,128)S(1)} %get-tuple-element.22.taps_ref), custom_call_target="tpu_custom_call" | custom-call | flops 2312110080 | bytes 1 | tf_op jit(solution)/shard_map/backward/pallas_call | solution.py:30
  28.0 2.4 %collective-permute-start.9 = (bf16[4,32,768]{2,1,0:T(8,128)(2,1)S(1)}, bf16[4,32,768]{2,1,0:T(8,128)(2,1)S(1)}, u32[]{:S(2)}, u32[]{:S(2)}) collective-permute-start(bf16[4,32,768]{2,1,0:T(8,128)(2,1)S(1)} %backward.5), channel_id=1, source_target_pairs={{0,3},{1,2},{2,1},{3,0},{4,7},{5,6},{6,5},{7,4},{8,11},{9,10},{10,... | collective-permute-start | bytes 589832 | tf_op jit(solution)/shard_map/ppermute | solution.py:382
  30.4 1.3 %backward.4 = bf16[4,32,768]{2,1,0:T(8,128)(2,1)S(1)} custom-call(f32[16,32,128]{2,1,0:T(8,128)S(1)} %get-tuple-element.34.valid_ref, f32[6,22,48,128]{3,2,1,0:T(8,128)S(1)} %project.1.grad_ref, f32[49,8,768]{2,1,0:T(8,128)S(1)} %get-tuple-element.22.taps_ref), custom_call_target="tpu_custom_call" | custom-call | flops 2312110080 | bytes 1 | tf_op jit(solution)/shard_map/backward/pallas_call | solution.py:30
  31.7 0.6 %collective-permute-start.8 = (bf16[4,32,768]{2,1,0:T(8,128)(2,1)S(1)}, bf16[4,32,768]{2,1,0:T(8,128)(2,1)S(1)}, u32[]{:S(2)}, u32[]{:S(2)}) collective-permute-start(bf16[4,32,768]{2,1,0:T(8,128)(2,1)S(1)} %backward.4), channel_id=1, source_target_pairs={{0,2},{1,3},{2,0},{3,1},{4,6},{5,7},{6,4},{7,5},{8,10},{9,11},{10,... | collective-permute-start | bytes 589832 | tf_op jit(solution)/shard_map/ppermute | solution.py:382
  32.3 2.7 %collective-permute-start.12 = (bf16[1,96,768]{2,1,0:T(8,128)(2,1)S(1)}, bf16[1,96,768]{2,1,0:T(8,128)(2,1)S(1)}, u32[]{:S(2)}, u32[]{:S(2)}) collective-permute-start(bf16[1,96,768]{2,1,0:T(8,128)(2,1)S(1)} %get-tuple-element.33), channel_id=1, source_target_pairs={{0,16},{4,20},{8,24},{12,28},{16,0},{20,4},{24,8},{28,12},{1,17},{... | collective-permute-start | bytes 442376 | tf_op jit(solution)/shard_map/ppermute | solution.py:424
  35.0 1.3 %backward.6 = bf16[4,32,768]{2,1,0:T(8,128)(2,1)S(1)} custom-call(f32[16,32,128]{2,1,0:T(8,128)S(1)} %get-tuple-element.34.valid_ref, f32[6,22,48,128]{3,2,1,0:T(8,128)S(1)} %project.1.grad_ref, f32[49,8,768]{2,1,0:T(8,128)S(1)} %get-tuple-element.22.taps_ref), custom_call_target="tpu_custom_call" | custom-call | flops 2312110080 | bytes 1 | tf_op jit(solution)/shard_map/backward/pallas_call | solution.py:30
  36.3 1.3 %collective-permute-start.11 = (bf16[4,32,768]{2,1,0:T(8,128)(2,1)S(1)}, bf16[4,32,768]{2,1,0:T(8,128)(2,1)S(1)}, u32[]{:S(2)}, u32[]{:S(2)}) collective-permute-start(bf16[4,32,768]{2,1,0:T(8,128)(2,1)S(1)} %backward.6), channel_id=1, source_target_pairs={{0,1},{1,0},{2,3},{3,2},{4,5},{5,4},{6,7},{7,6},{8,9},{9,8},{10,11... | collective-permute-start | bytes 589832 | tf_op jit(solution)/shard_map/ppermute | solution.py:382
  37.6 1.3 %backward.7.refs_3_ = f32[4,32,768]{2,1,0:T(8,128)S(1)} custom-call(f32[16,32,128]{2,1,0:T(8,128)S(1)} %get-tuple-element.34.valid_ref, f32[6,22,48,128]{3,2,1,0:T(8,128)S(1)} %project.1.grad_ref, f32[49,8,768]{2,1,0:T(8,128)S(1)} %get-tuple-element.22.taps_ref), custom_call_target="tpu_custom_call" | custom-call | flops 2312110080 | bytes 1 | tf_op jit(solution)/shard_map/backward/pallas_call | solution.py:30
  38.9 1.2 %collective-permute-done.8.refs_0_ = bf16[4,32,768]{2,1,0:T(8,128)(2,1)S(1)} collective-permute-done((bf16[4,32,768]{2,1,0:T(8,128)(2,1)S(1)}, bf16[4,32,768]{2,1,0:T(8,128)(2,1)S(1)}, u32[]{:S(2)}, u32[]{:S(2)}) %collective-permute-start.8) | collective-permute-done | bytes 196640 | tf_op jit(solution)/shard_map/ppermute | solution.py:382
  40.1 1.7 %collective-permute-done.12 = bf16[1,96,768]{2,1,0:T(8,128)(2,1)S(1)} collective-permute-done((bf16[1,96,768]{2,1,0:T(8,128)(2,1)S(1)}, bf16[1,96,768]{2,1,0:T(8,128)(2,1)S(1)}, u32[]{:S(2)}, u32[]{:S(2)}) %collective-permute-start.12) | collective-permute-done | bytes 147488 | tf_op jit(solution)/shard_map/ppermute | solution.py:424
  41.7 0.5 %collective-permute-done.11.refs_2_ = bf16[4,32,768]{2,1,0:T(8,128)(2,1)S(1)} collective-permute-done((bf16[4,32,768]{2,1,0:T(8,128)(2,1)S(1)}, bf16[4,32,768]{2,1,0:T(8,128)(2,1)S(1)}, u32[]{:S(2)}, u32[]{:S(2)}) %collective-permute-start.11) | collective-permute-done | bytes 196640 | tf_op jit(solution)/shard_map/ppermute | solution.py:382
  42.3 0.9 %finish.1 = (bf16[4,32,768]{2,1,0:T(8,128)(2,1)}, f32[96,768]{1,0:T(8,128)}) custom-call(bf16[4,32,768]{2,1,0:T(8,128)(2,1)S(1)} %collective-permute-done.8.refs_0_, bf16[4,32,768]{2,1,0:T(8,128)(2,1)S(1)} %collective-permute-done.9.refs_1_, bf16[4,32,768]{2,1,0:T(8,128)(2,1)S(1)} %collective-permute-done.11.refs_2_, f32[4,32,768]{2,1,0:T(8,128)S(1)} %backward.7.refs_3_, ...), custom_call_target="tpu_custom_call" | custom-call | flops 1 | bytes 1 | tf_op jit(solution)/shard_map/finish/pallas_call | solution.py:30
  (29 shorter events, 1.4 us)
Async XLA Ops:
  0.6 10.5 %copy-start.1 = (bf16[1,4,32,768]{3,2,1,0:T(8,128)(2,1)S(1)}, bf16[1,4,32,768]{3,2,1,0:T(8,128)(2,1)}, u32[]{:S(2)}) copy-start(bf16[1,4,32,768]{3,2,1,0:T(8,128)(2,1)} %param.8) | copy-start | bytes 589828
  0.6 10.5 %copy-start.3 = (bf16[49,768]{1,0:T(8,128)(2,1)S(1)}, bf16[49,768]{1,0:T(8,128)(2,1)}, u32[]{:S(2)}) copy-start(bf16[49,768]{1,0:T(8,128)(2,1)} %taps_ref.1) | copy-start | bytes 225796
  0.7 10.7 %collective-permute-start.3 = (bf16[4,32,768]{2,1,0:T(8,128)(2,1)}, bf16[4,32,768]{2,1,0:T(8,128)(2,1)S(1)}, u32[]{:S(2)}, u32[]{:S(2)}) collective-permute-start(bf16[4,32,768]{2,1,0:T(8,128)(2,1)} %bitcast.10), channel_id=1, source_target_pairs={{0,1},{1,0},{2,3},{3,2},{4,5},{5,4},{6,7},{7,6},{8,9},{9,8},{10,11... | collective-permute-start | bytes 589832 | tf_op jit(solution)/shard_map/ppermute | solution.py:382
  3.7 10.8 %collective-permute-start.1 = (bf16[4,32,768]{2,1,0:T(8,128)(2,1)}, bf16[4,32,768]{2,1,0:T(8,128)(2,1)S(1)}, u32[]{:S(2)}, u32[]{:S(2)}) collective-permute-start(bf16[4,32,768]{2,1,0:T(8,128)(2,1)} %bitcast.11), channel_id=1, source_target_pairs={{0,2},{1,3},{2,0},{3,1},{4,6},{5,7},{6,4},{7,5},{8,10},{9,11},{10,... | collective-permute-start | bytes 589832 | tf_op jit(solution)/shard_map/ppermute | solution.py:382
  5.2 9.3 %collective-permute-start.2 = (bf16[4,32,768]{2,1,0:T(8,128)(2,1)}, bf16[4,32,768]{2,1,0:T(8,128)(2,1)S(1)}, u32[]{:S(2)}, u32[]{:S(2)}) collective-permute-start(bf16[4,32,768]{2,1,0:T(8,128)(2,1)} %bitcast.12), channel_id=1, source_target_pairs={{0,3},{1,2},{2,1},{3,0},{4,7},{5,6},{6,5},{7,4},{8,11},{9,10},{10,... | collective-permute-start | bytes 589832 | tf_op jit(solution)/shard_map/ppermute | solution.py:382
  5.2 13.8 %collective-permute-start = (bf16[96,768]{1,0:T(8,128)(2,1)}, bf16[96,768]{1,0:T(8,128)(2,1)S(1)}, u32[]{:S(2)}, u32[]{:S(2)}) collective-permute-start(bf16[96,768]{1,0:T(8,128)(2,1)} %refs_0_.1), channel_id=1, source_target_pairs={{0,8},{4,12},{8,0},{12,4},{16,24},{20,28},{24,16},{28,20},{1,9},{5... | collective-permute-start | bytes 442376 | tf_op jit(solution)/shard_map/ppermute | solution.py:388
  7.2 10.1 %collective-permute-start.5 = (bf16[96,768]{1,0:T(8,128)(2,1)}, bf16[96,768]{1,0:T(8,128)(2,1)S(1)}, u32[]{:S(2)}, u32[]{:S(2)}) collective-permute-start(bf16[96,768]{1,0:T(8,128)(2,1)} %refs_0_.1), channel_id=1, source_target_pairs={{0,16},{4,20},{8,24},{12,28},{16,0},{20,4},{24,8},{28,12},{1,17},{... | collective-permute-start | bytes 442376 | tf_op jit(solution)/shard_map/ppermute | solution.py:388
  14.2 4.7 %copy-start.4 = (f32[768]{0:T(1024)S(1)}, f32[768]{0:T(1024)}, u32[]{:S(2)}) copy-start(f32[768]{0:T(1024)} %param.12) | copy-start | bytes 9220
  14.3 4.7 %copy-start.5 = (f32[768]{0:T(1024)S(1)}, f32[768]{0:T(1024)}, u32[]{:S(2)}) copy-start(f32[768]{0:T(1024)} %param.13) | copy-start | bytes 9220
  17.3 2.6 %copy-start = (bf16[1,16,32,768]{3,2,1,0:T(8,128)(2,1)S(1)}, bf16[1,16,32,768]{3,2,1,0:T(8,128)(2,1)}, u32[]{:S(2)}) copy-start(bf16[1,16,32,768]{3,2,1,0:T(8,128)(2,1)} %param.9) | copy-start | bytes 2359300
  17.3 5.2 %copy-start.2 = (bf16[96,768]{1,0:T(8,128)(2,1)S(1)}, bf16[96,768]{1,0:T(8,128)(2,1)}, u32[]{:S(2)}) copy-start(bf16[96,768]{1,0:T(8,128)(2,1)} %refs_0_.1) | copy-start | bytes 442372
  17.3 5.2 %collective-permute-start.6 = (bf16[96,768]{1,0:T(8,128)(2,1)S(1)}, bf16[96,768]{1,0:T(8,128)(2,1)S(1)}, u32[]{:S(2)}, u32[]{:S(2)}) collective-permute-start(bf16[96,768]{1,0:T(8,128)(2,1)S(1)} %collective-permute-done.5.refs_2_), channel_id=1, source_target_pairs={{0,8},{4,12},{8,0},{12,4},{16,24},{20,28},{24,16},{28,20},{1,9},{5... | collective-permute-start | bytes 442376 | tf_op jit(solution)/shard_map/ppermute | solution.py:388
  21.0 2.1 %collective-permute-start.4 = (bf16[4,96,768]{2,1,0:T(8,128)(2,1)S(1)}, bf16[4,96,768]{2,1,0:T(8,128)(2,1)S(1)}, u32[]{:S(2)}, u32[]{:S(2)}) collective-permute-start(bf16[4,96,768]{2,1,0:T(8,128)(2,1)S(1)} %get-tuple-element.25), channel_id=1, source_target_pairs={{0,4},{4,0},{8,12},{12,8},{16,20},{20,16},{24,28},{28,24},{1,5},{5... | collective-permute-start | bytes 1769480 | tf_op jit(solution)/shard_map/ppermute | solution.py:424
  22.6 2.1 %collective-permute-start.7 = (bf16[4,96,768]{2,1,0:T(8,128)(2,1)S(1)}, bf16[4,96,768]{2,1,0:T(8,128)(2,1)S(1)}, u32[]{:S(2)}, u32[]{:S(2)}) collective-permute-start(bf16[4,96,768]{2,1,0:T(8,128)(2,1)S(1)} %stack.1.refs_0_), channel_id=1, source_target_pairs={{0,4},{4,0},{8,12},{12,8},{16,20},{20,16},{24,28},{28,24},{1,5},{5... | collective-permute-start | bytes 1769480 | tf_op jit(solution)/shard_map/ppermute | solution.py:375
  23.2 9.1 %collective-permute-start.10 = (bf16[2,96,768]{2,1,0:T(8,128)(2,1)S(1)}, bf16[2,96,768]{2,1,0:T(8,128)(2,1)S(1)}, u32[]{:S(2)}, u32[]{:S(2)}) collective-permute-start(bf16[2,96,768]{2,1,0:T(8,128)(2,1)S(1)} %get-tuple-element.26), channel_id=1, source_target_pairs={{0,8},{4,12},{8,0},{12,4},{16,24},{20,28},{24,16},{28,20},{1,9},{5... | collective-permute-start | bytes 884744 | tf_op jit(solution)/shard_map/ppermute | solution.py:424
  28.0 11.0 %collective-permute-start.9 = (bf16[4,32,768]{2,1,0:T(8,128)(2,1)S(1)}, bf16[4,32,768]{2,1,0:T(8,128)(2,1)S(1)}, u32[]{:S(2)}, u32[]{:S(2)}) collective-permute-start(bf16[4,32,768]{2,1,0:T(8,128)(2,1)S(1)} %backward.5), channel_id=1, source_target_pairs={{0,3},{1,2},{2,1},{3,0},{4,7},{5,6},{6,5},{7,4},{8,11},{9,10},{10,... | collective-permute-start | bytes 589832 | tf_op jit(solution)/shard_map/ppermute | solution.py:382
  31.7 8.4 %collective-permute-start.8 = (bf16[4,32,768]{2,1,0:T(8,128)(2,1)S(1)}, bf16[4,32,768]{2,1,0:T(8,128)(2,1)S(1)}, u32[]{:S(2)}, u32[]{:S(2)}) collective-permute-start(bf16[4,32,768]{2,1,0:T(8,128)(2,1)S(1)} %backward.4), channel_id=1, source_target_pairs={{0,2},{1,3},{2,0},{3,1},{4,6},{5,7},{6,4},{7,5},{8,10},{9,11},{10,... | collective-permute-start | bytes 589832 | tf_op jit(solution)/shard_map/ppermute | solution.py:382
  32.3 9.4 %collective-permute-start.12 = (bf16[1,96,768]{2,1,0:T(8,128)(2,1)S(1)}, bf16[1,96,768]{2,1,0:T(8,128)(2,1)S(1)}, u32[]{:S(2)}, u32[]{:S(2)}) collective-permute-start(bf16[1,96,768]{2,1,0:T(8,128)(2,1)S(1)} %get-tuple-element.33), channel_id=1, source_target_pairs={{0,16},{4,20},{8,24},{12,28},{16,0},{20,4},{24,8},{28,12},{1,17},{... | collective-permute-start | bytes 442376 | tf_op jit(solution)/shard_map/ppermute | solution.py:424
  36.3 6.0 %collective-permute-start.11 = (bf16[4,32,768]{2,1,0:T(8,128)(2,1)S(1)}, bf16[4,32,768]{2,1,0:T(8,128)(2,1)S(1)}, u32[]{:S(2)}, u32[]{:S(2)}) collective-permute-start(bf16[4,32,768]{2,1,0:T(8,128)(2,1)S(1)} %backward.6), channel_id=1, source_target_pairs={{0,1},{1,0},{2,3},{3,2},{4,5},{5,4},{6,7},{7,6},{8,9},{9,8},{10,11... | collective-permute-start | bytes 589832 | tf_op jit(solution)/shard_map/ppermute | solution.py:382

commit v2 on v0

--- a/solution.py
+++ b/solution.py
@@ -457,8 +457,8 @@
     half = bands // 2
     mixed = forward(valid, wide, acts[:half], range(half), bands)
     sent = send_pieces(proj_weight)
+    proj_mine = stack(gather_pairs(proj_weight, sent, mixed))
     mixed = forward(valid, wide, acts[half:], range(half, bands), bands, mixed)
-    proj_mine = stack(gather_pairs(proj_weight, sent, mixed))
 
     normed, centres, spreads = normalise(after(valid, sent[1]), mixed, gain, shift)
     whole, send = outer(normed, grad, count)

time: 43.2 us -> 43.3 us (level)
  waiting for transfers between devices: 5.86 us -> 4.94 us
  starting transfers between devices: 19.1 us -> 19.9 us
    ppermute x3, waiting for transfers between devices: 2.06 us -> 3.69 us  [scatter_section(): got = lax.ppermute(send, 'section', way)]
    ppermute x6, waiting for transfers between devices: 2.1 us -> 0.74 us  [send_rows(): lax.ppermute(value, 'rows', [(i, partner(i, index, count)) for i in range...]
    ppermute x3, waiting for transfers between devices: 1.51 us -> 0.51 us  [send_section(): return lax.ppermute(value, 'section', way)]
    ppermute x3, starting transfers between devices: 6.26 us -> 5.4 us  [send_section(): return lax.ppermute(value, 'section', way)]
    ppermute x3, starting transfers between devices: 4.04 us -> 4.72 us  [scatter_section(): got = lax.ppermute(send, 'section', way)]
    ppermute x6, starting transfers between devices: 8.7 us -> 9.26 us  [send_rows(): lax.ppermute(value, 'rows', [(i, partner(i, index, count)) for i in range...]
    ppermute x1, starting transfers between devices: 0.07 us -> 0.54 us  [swap_pairs(): return lax.ppermute(value, 'section', [(i, i ^ 1) for i in range(count)])]
  transfers between devices with their start and end apart: 13 -> 13, of which waited for: 8 -> 4; matrix products, arithmetic and copies ran while one was open for 0% -> 0% of each run, Pallas kernels for 35% -> 35%
where the time goes in v2:
time: 43.3 us; the launch traced here: 43.1 us
  starting transfers between devices  19.9 us (46%)
  Pallas kernels  15.9 us (37%)
  waiting for transfers between devices  4.94 us (11%)
  between operations  2.13 us (5%)
    pallas_call x15, Pallas kernels, run(): pl.pallas_call(kernel, out_shape=tuple(outs), in_specs=[smem if arg.dtype...  15.9 us
    ppermute x6, starting transfers between devices, send_rows(): lax.ppermute(value, 'rows', [(i, partner(i, index, count)) for i in range...  9.26 us
    ppermute x3, starting transfers between devices, send_section(): return lax.ppermute(value, 'section', way)  5.4 us
    ppermute x3, starting transfers between devices, scatter_section(): got = lax.ppermute(send, 'section', way)  4.72 us
    ppermute x3, waiting for transfers between devices, scatter_section(): got = lax.ppermute(send, 'section', way)  3.69 us
  transfers between devices with their start and end apart: 13, of which 4 were waited for; matrix products, arithmetic and copies ran while one was open for 0% of the time, Pallas kernels for 35%

profile of v2, /device:TPU:0, one launch (start us, length us, event | category | flops | bytes accessed | tf_op | source)
XLA Modules:
  0.0 43.1 jit_solution(6208456071672562662)
XLA Ops:
  0.7 3.0 %collective-permute-start.3 = (bf16[4,32,768]{2,1,0:T(8,128)(2,1)}, bf16[4,32,768]{2,1,0:T(8,128)(2,1)S(1)}, u32[]{:S(2)}, u32[]{:S(2)}) collective-permute-start(bf16[4,32,768]{2,1,0:T(8,128)(2,1)} %bitcast.10), channel_id=1, source_target_pairs={{0,1},{1,0},{2,3},{3,2},{4,5},{5,4},{6,7},{7,6},{8,9},{9,8},{10,11... | collective-permute-start | bytes 589832 | tf_op jit(solution)/shard_map/ppermute | solution.py:381
  3.7 1.5 %collective-permute-start.1 = (bf16[4,32,768]{2,1,0:T(8,128)(2,1)}, bf16[4,32,768]{2,1,0:T(8,128)(2,1)S(1)}, u32[]{:S(2)}, u32[]{:S(2)}) collective-permute-start(bf16[4,32,768]{2,1,0:T(8,128)(2,1)} %bitcast.11), channel_id=1, source_target_pairs={{0,2},{1,3},{2,0},{3,1},{4,6},{5,7},{6,4},{7,5},{8,10},{9,11},{10,... | collective-permute-start | bytes 589832 | tf_op jit(solution)/shard_map/ppermute | solution.py:381
  5.2 3.0 %collective-permute-start.5 = (bf16[96,768]{1,0:T(8,128)(2,1)}, bf16[96,768]{1,0:T(8,128)(2,1)S(1)}, u32[]{:S(2)}, u32[]{:S(2)}) collective-permute-start(bf16[96,768]{1,0:T(8,128)(2,1)} %refs_0_.1), channel_id=1, source_target_pairs={{0,16},{4,20},{8,24},{12,28},{16,0},{20,4},{24,8},{28,12},{1,17},{... | collective-permute-start | bytes 442376 | tf_op jit(solution)/shard_map/ppermute | solution.py:387
  8.2 1.6 %collective-permute-start = (bf16[96,768]{1,0:T(8,128)(2,1)}, bf16[96,768]{1,0:T(8,128)(2,1)S(1)}, u32[]{:S(2)}, u32[]{:S(2)}) collective-permute-start(bf16[96,768]{1,0:T(8,128)(2,1)} %refs_0_.1), channel_id=1, source_target_pairs={{0,8},{4,12},{8,0},{12,4},{16,24},{20,28},{24,16},{28,20},{1,9},{5... | collective-permute-start | bytes 442376 | tf_op jit(solution)/shard_map/ppermute | solution.py:387
  11.4 2.7 %forward.2.refs_2_ = f32[6,22,32,128]{3,2,1,0:T(8,128)S(1)} custom-call(f32[16,32,128]{2,1,0:T(8,128)S(1)} %get-tuple-element.34.valid_ref, f32[49,8,768]{2,1,0:T(8,128)S(1)} %get-tuple-element.22.taps_ref, bf16[4,32,768]{2,1,0:T(8,128)(2,1)S(1)} %bitcast.14, bf16[4,32,768]{2,1,0:T(8,128)(2,1)S(1)} %collective-permute-done.3.refs_1_), custom_call_target="tpu_custom_call" | custom-call | flops 13872660480 | bytes 1 | tf_op jit(solution)/shard_map/forward/pallas_call | solution.py:29
  14.7 0.8 %collective-permute-start.6 = (bf16[96,768]{1,0:T(8,128)(2,1)S(1)}, bf16[96,768]{1,0:T(8,128)(2,1)S(1)}, u32[]{:S(2)}, u32[]{:S(2)}) collective-permute-start(bf16[96,768]{1,0:T(8,128)(2,1)S(1)} %collective-permute-done.5.refs_2_), channel_id=1, source_target_pairs={{0,8},{4,12},{8,0},{12,4},{16,24},{20,28},{24,16},{28,20},{1,9},{5... | collective-permute-start | bytes 442376 | tf_op jit(solution)/shard_map/ppermute | solution.py:387
  15.5 2.7 %forward.3.mixed = f32[6,22,32,128]{3,2,1,0:T(8,128)S(1)} custom-call(f32[16,32,128]{2,1,0:T(8,128)S(1)} %get-tuple-element.34.valid_ref, f32[49,8,768]{2,1,0:T(8,128)S(1)} %get-tuple-element.22.taps_ref, bf16[4,32,768]{2,1,0:T(8,128)(2,1)S(1)} %collective-permute-done.1.refs_0_, ...), custom_call_target="tpu_custom_call", output_to_operand_aliasing={{}: (4, {})} | custom-call | flops 1 | bytes 1 | tf_op jit(solution)/shard_map/forward/pallas_call | solution.py:29
  18.2 0.9 %normalise.1 = (bf16[512,768]{1,0:T(8,128)(2,1)S(1)}, f32[16,32,128]{2,1,0:T(8,128)S(1)}, f32[16,32,128]{2,1,0:T(8,128)S(1)}) custom-call(f32[16,32,128]{2,1,0:T(8,128)S(1)} %get-tuple-element.34.valid_ref, f32[6,22,32,128]{3,2,1,0:T(8,128)S(1)} %forward.3.mixed, f32[6,128]{1,0:T(8,128)S(1)} %bitcast.16, f32[6,128]{1,0:T(8,128)S(1)} %bitcast.18), custom_call_target="tpu_custom_call" | custom-call | flops 1 | bytes 1 | tf_op jit(solution)/shard_map/normalise/pallas_call | solution.py:29
  19.3 1.0 %outer.1 = (f32[8,96,768]{2,1,0:T(8,128)S(1)}, bf16[4,96,768]{2,1,0:T(8,128)(2,1)S(1)}) custom-call(bf16[512,768]{1,0:T(8,128)(2,1)S(1)} %get-tuple-element.23.normed_ref, bf16[512,768]{1,0:T(8,128)(2,1)S(1)} %bitcast.7), custom_call_target="tpu_custom_call" | custom-call | flops 1 | bytes 1 | tf_op jit(solution)/shard_map/outer/pallas_call | solution.py:29
  20.5 0.5 %collective-permute-start.7 = (bf16[4,96,768]{2,1,0:T(8,128)(2,1)S(1)}, bf16[4,96,768]{2,1,0:T(8,128)(2,1)S(1)}, u32[]{:S(2)}, u32[]{:S(2)}) collective-permute-start(bf16[4,96,768]{2,1,0:T(8,128)(2,1)S(1)} %stack.1.refs_0_), channel_id=1, source_target_pairs={{0,4},{4,0},{8,12},{12,8},{16,20},{20,16},{24,28},{28,24},{1,5},{5... | collective-permute-start | bytes 1769480 | tf_op jit(solution)/shard_map/ppermute | solution.py:374
  21.0 1.4 %collective-permute-done.4.got_ref = bf16[4,96,768]{2,1,0:T(8,128)(2,1)S(1)} collective-permute-done((bf16[4,96,768]{2,1,0:T(8,128)(2,1)S(1)}, bf16[4,96,768]{2,1,0:T(8,128)(2,1)S(1)}, u32[]{:S(2)}, u32[]{:S(2)}) %collective-permute-start.4) | collective-permute-done | bytes 589856 | tf_op jit(solution)/shard_map/ppermute | solution.py:423
  22.5 1.3 %collective-permute-start.10 = (bf16[2,96,768]{2,1,0:T(8,128)(2,1)S(1)}, bf16[2,96,768]{2,1,0:T(8,128)(2,1)S(1)}, u32[]{:S(2)}, u32[]{:S(2)}) collective-permute-start(bf16[2,96,768]{2,1,0:T(8,128)(2,1)S(1)} %get-tuple-element.26), channel_id=1, source_target_pairs={{0,8},{4,12},{8,0},{12,4},{16,24},{20,28},{24,16},{28,20},{1,9},{5... | collective-permute-start | bytes 884744 | tf_op jit(solution)/shard_map/ppermute | solution.py:423
  23.8 2.0 %project.1.grad_ref = f32[6,22,48,128]{3,2,1,0:T(8,128)S(1)} custom-call(f32[16,32,128]{2,1,0:T(8,128)S(1)} %get-tuple-element.34.valid_ref, bf16[512,768]{1,0:T(8,128)(2,1)S(1)} %bitcast.8, f32[6,22,32,128]{3,2,1,0:T(8,128)S(1)} %forward.3.mixed, f32[16,32,128]{2,1,0:T(8,128)S(1)} %get-tuple-element.29.centres, ...), custom_call_target="tpu_custom_call" | custom-call | flops 1557135360 | bytes 4325376 | tf_op jit(solution)/shard_map/project/pallas_call | solution.py:29
  25.8 1.3 %backward.5 = bf16[4,32,768]{2,1,0:T(8,128)(2,1)S(1)} custom-call(f32[16,32,128]{2,1,0:T(8,128)S(1)} %get-tuple-element.34.valid_ref, f32[6,22,48,128]{3,2,1,0:T(8,128)S(1)} %project.1.grad_ref, f32[49,8,768]{2,1,0:T(8,128)S(1)} %get-tuple-element.22.taps_ref), custom_call_target="tpu_custom_call" | custom-call | flops 2312110080 | bytes 1 | tf_op jit(solution)/shard_map/backward/pallas_call | solution.py:29
  27.1 2.6 %collective-permute-start.9 = (bf16[4,32,768]{2,1,0:T(8,128)(2,1)S(1)}, bf16[4,32,768]{2,1,0:T(8,128)(2,1)S(1)}, u32[]{:S(2)}, u32[]{:S(2)}) collective-permute-start(bf16[4,32,768]{2,1,0:T(8,128)(2,1)S(1)} %backward.5), channel_id=1, source_target_pairs={{0,3},{1,2},{2,1},{3,0},{4,7},{5,6},{6,5},{7,4},{8,11},{9,10},{10,... | collective-permute-start | bytes 589832 | tf_op jit(solution)/shard_map/ppermute | solution.py:381
  29.7 1.3 %backward.4 = bf16[4,32,768]{2,1,0:T(8,128)(2,1)S(1)} custom-call(f32[16,32,128]{2,1,0:T(8,128)S(1)} %get-tuple-element.34.valid_ref, f32[6,22,48,128]{3,2,1,0:T(8,128)S(1)} %project.1.grad_ref, f32[49,8,768]{2,1,0:T(8,128)S(1)} %get-tuple-element.22.taps_ref), custom_call_target="tpu_custom_call" | custom-call | flops 2312110080 | bytes 1 | tf_op jit(solution)/shard_map/backward/pallas_call | solution.py:29
  31.0 0.6 %collective-permute-start.8 = (bf16[4,32,768]{2,1,0:T(8,128)(2,1)S(1)}, bf16[4,32,768]{2,1,0:T(8,128)(2,1)S(1)}, u32[]{:S(2)}, u32[]{:S(2)}) collective-permute-start(bf16[4,32,768]{2,1,0:T(8,128)(2,1)S(1)} %backward.4), channel_id=1, source_target_pairs={{0,2},{1,3},{2,0},{3,1},{4,6},{5,7},{6,4},{7,5},{8,10},{9,11},{10,... | collective-permute-start | bytes 589832 | tf_op jit(solution)/shard_map/ppermute | solution.py:381
  31.7 3.3 %collective-permute-start.12 = (bf16[1,96,768]{2,1,0:T(8,128)(2,1)S(1)}, bf16[1,96,768]{2,1,0:T(8,128)(2,1)S(1)}, u32[]{:S(2)}, u32[]{:S(2)}) collective-permute-start(bf16[1,96,768]{2,1,0:T(8,128)(2,1)S(1)} %get-tuple-element.33), channel_id=1, source_target_pairs={{0,16},{4,20},{8,24},{12,28},{16,0},{20,4},{24,8},{28,12},{1,17},{... | collective-permute-start | bytes 442376 | tf_op jit(solution)/shard_map/ppermute | solution.py:423
  35.0 1.3 %backward.6 = bf16[4,32,768]{2,1,0:T(8,128)(2,1)S(1)} custom-call(f32[16,32,128]{2,1,0:T(8,128)S(1)} %get-tuple-element.34.valid_ref, f32[6,22,48,128]{3,2,1,0:T(8,128)S(1)} %project.1.grad_ref, f32[49,8,768]{2,1,0:T(8,128)S(1)} %get-tuple-element.22.taps_ref), custom_call_target="tpu_custom_call" | custom-call | flops 2312110080 | bytes 1 | tf_op jit(solution)/shard_map/backward/pallas_call | solution.py:29
  36.3 1.6 %collective-permute-start.11 = (bf16[4,32,768]{2,1,0:T(8,128)(2,1)S(1)}, bf16[4,32,768]{2,1,0:T(8,128)(2,1)S(1)}, u32[]{:S(2)}, u32[]{:S(2)}) collective-permute-start(bf16[4,32,768]{2,1,0:T(8,128)(2,1)S(1)} %backward.6), channel_id=1, source_target_pairs={{0,1},{1,0},{2,3},{3,2},{4,5},{5,4},{6,7},{7,6},{8,9},{9,8},{10,11... | collective-permute-start | bytes 589832 | tf_op jit(solution)/shard_map/ppermute | solution.py:381
  37.9 1.3 %backward.7.refs_3_ = f32[4,32,768]{2,1,0:T(8,128)S(1)} custom-call(f32[16,32,128]{2,1,0:T(8,128)S(1)} %get-tuple-element.34.valid_ref, f32[6,22,48,128]{3,2,1,0:T(8,128)S(1)} %project.1.grad_ref, f32[49,8,768]{2,1,0:T(8,128)S(1)} %get-tuple-element.22.taps_ref), custom_call_target="tpu_custom_call" | custom-call | flops 2312110080 | bytes 1 | tf_op jit(solution)/shard_map/backward/pallas_call | solution.py:29
  39.2 2.3 %collective-permute-done.12 = bf16[1,96,768]{2,1,0:T(8,128)(2,1)S(1)} collective-permute-done((bf16[1,96,768]{2,1,0:T(8,128)(2,1)S(1)}, bf16[1,96,768]{2,1,0:T(8,128)(2,1)S(1)}, u32[]{:S(2)}, u32[]{:S(2)}) %collective-permute-start.12) | collective-permute-done | bytes 147488 | tf_op jit(solution)/shard_map/ppermute | solution.py:423
  41.5 0.7 %collective-permute-done.11.refs_2_ = bf16[4,32,768]{2,1,0:T(8,128)(2,1)S(1)} collective-permute-done((bf16[4,32,768]{2,1,0:T(8,128)(2,1)S(1)}, bf16[4,32,768]{2,1,0:T(8,128)(2,1)S(1)}, u32[]{:S(2)}, u32[]{:S(2)}) %collective-permute-start.11) | collective-permute-done | bytes 196640 | tf_op jit(solution)/shard_map/ppermute | solution.py:381
  42.2 0.9 %finish.1 = (bf16[4,32,768]{2,1,0:T(8,128)(2,1)}, f32[96,768]{1,0:T(8,128)}) custom-call(bf16[4,32,768]{2,1,0:T(8,128)(2,1)S(1)} %collective-permute-done.8.refs_0_, bf16[4,32,768]{2,1,0:T(8,128)(2,1)S(1)} %collective-permute-done.9.refs_1_, bf16[4,32,768]{2,1,0:T(8,128)(2,1)S(1)} %collective-permute-done.11.refs_2_, f32[4,32,768]{2,1,0:T(8,128)S(1)} %backward.7.refs_3_, ...), custom_call_target="tpu_custom_call" | custom-call | flops 1 | bytes 1 | tf_op jit(solution)/shard_map/finish/pallas_call | solution.py:29
  (29 shorter events, 1.3 us)
Async XLA Ops:
  0.6 10.5 %copy-start.1 = (bf16[1,4,32,768]{3,2,1,0:T(8,128)(2,1)S(1)}, bf16[1,4,32,768]{3,2,1,0:T(8,128)(2,1)}, u32[]{:S(2)}) copy-start(bf16[1,4,32,768]{3,2,1,0:T(8,128)(2,1)} %param.8) | copy-start | bytes 589828
  0.6 10.5 %copy-start.3 = (bf16[49,768]{1,0:T(8,128)(2,1)S(1)}, bf16[49,768]{1,0:T(8,128)(2,1)}, u32[]{:S(2)}) copy-start(bf16[49,768]{1,0:T(8,128)(2,1)} %taps_ref.1) | copy-start | bytes 225796
  0.7 10.7 %collective-permute-start.3 = (bf16[4,32,768]{2,1,0:T(8,128)(2,1)}, bf16[4,32,768]{2,1,0:T(8,128)(2,1)S(1)}, u32[]{:S(2)}, u32[]{:S(2)}) collective-permute-start(bf16[4,32,768]{2,1,0:T(8,128)(2,1)} %bitcast.10), channel_id=1, source_target_pairs={{0,1},{1,0},{2,3},{3,2},{4,5},{5,4},{6,7},{7,6},{8,9},{9,8},{10,11... | collective-permute-start | bytes 589832 | tf_op jit(solution)/shard_map/ppermute | solution.py:381
  3.7 11.8 %collective-permute-start.1 = (bf16[4,32,768]{2,1,0:T(8,128)(2,1)}, bf16[4,32,768]{2,1,0:T(8,128)(2,1)S(1)}, u32[]{:S(2)}, u32[]{:S(2)}) collective-permute-start(bf16[4,32,768]{2,1,0:T(8,128)(2,1)} %bitcast.11), channel_id=1, source_target_pairs={{0,2},{1,3},{2,0},{3,1},{4,6},{5,7},{6,4},{7,5},{8,10},{9,11},{10,... | collective-permute-start | bytes 589832 | tf_op jit(solution)/shard_map/ppermute | solution.py:381
  5.2 10.3 %collective-permute-start.2 = (bf16[4,32,768]{2,1,0:T(8,128)(2,1)}, bf16[4,32,768]{2,1,0:T(8,128)(2,1)S(1)}, u32[]{:S(2)}, u32[]{:S(2)}) collective-permute-start(bf16[4,32,768]{2,1,0:T(8,128)(2,1)} %bitcast.12), channel_id=1, source_target_pairs={{0,3},{1,2},{2,1},{3,0},{4,7},{5,6},{6,5},{7,4},{8,11},{9,10},{10,... | collective-permute-start | bytes 589832 | tf_op jit(solution)/shard_map/ppermute | solution.py:381
  5.2 9.5 %collective-permute-start.5 = (bf16[96,768]{1,0:T(8,128)(2,1)}, bf16[96,768]{1,0:T(8,128)(2,1)S(1)}, u32[]{:S(2)}, u32[]{:S(2)}) collective-permute-start(bf16[96,768]{1,0:T(8,128)(2,1)} %refs_0_.1), channel_id=1, source_target_pairs={{0,16},{4,20},{8,24},{12,28},{16,0},{20,4},{24,8},{28,12},{1,17},{... | collective-permute-start | bytes 442376 | tf_op jit(solution)/shard_map/ppermute | solution.py:387
  8.2 7.2 %collective-permute-start = (bf16[96,768]{1,0:T(8,128)(2,1)}, bf16[96,768]{1,0:T(8,128)(2,1)S(1)}, u32[]{:S(2)}, u32[]{:S(2)}) collective-permute-start(bf16[96,768]{1,0:T(8,128)(2,1)} %refs_0_.1), channel_id=1, source_target_pairs={{0,8},{4,12},{8,0},{12,4},{16,24},{20,28},{24,16},{28,20},{1,9},{5... | collective-permute-start | bytes 442376 | tf_op jit(solution)/shard_map/ppermute | solution.py:387
  14.1 4.1 %copy-start.4 = (f32[768]{0:T(1024)S(1)}, f32[768]{0:T(1024)}, u32[]{:S(2)}) copy-start(f32[768]{0:T(1024)} %param.12) | copy-start | bytes 9220
  14.2 4.1 %copy-start.5 = (f32[768]{0:T(1024)S(1)}, f32[768]{0:T(1024)}, u32[]{:S(2)}) copy-start(f32[768]{0:T(1024)} %param.13) | copy-start | bytes 9220
  14.7 5.7 %collective-permute-start.6 = (bf16[96,768]{1,0:T(8,128)(2,1)S(1)}, bf16[96,768]{1,0:T(8,128)(2,1)S(1)}, u32[]{:S(2)}, u32[]{:S(2)}) collective-permute-start(bf16[96,768]{1,0:T(8,128)(2,1)S(1)} %collective-permute-done.5.refs_2_), channel_id=1, source_target_pairs={{0,8},{4,12},{8,0},{12,4},{16,24},{20,28},{24,16},{28,20},{1,9},{5... | collective-permute-start | bytes 442376 | tf_op jit(solution)/shard_map/ppermute | solution.py:387
  18.2 1.1 %copy-start = (bf16[1,16,32,768]{3,2,1,0:T(8,128)(2,1)S(1)}, bf16[1,16,32,768]{3,2,1,0:T(8,128)(2,1)}, u32[]{:S(2)}) copy-start(bf16[1,16,32,768]{3,2,1,0:T(8,128)(2,1)} %param.9) | copy-start | bytes 2359300
  18.2 2.2 %copy-start.2 = (bf16[96,768]{1,0:T(8,128)(2,1)S(1)}, bf16[96,768]{1,0:T(8,128)(2,1)}, u32[]{:S(2)}) copy-start(bf16[96,768]{1,0:T(8,128)(2,1)} %refs_0_.1) | copy-start | bytes 442372
  20.3 2.1 %collective-permute-start.4 = (bf16[4,96,768]{2,1,0:T(8,128)(2,1)S(1)}, bf16[4,96,768]{2,1,0:T(8,128)(2,1)S(1)}, u32[]{:S(2)}, u32[]{:S(2)}) collective-permute-start(bf16[4,96,768]{2,1,0:T(8,128)(2,1)S(1)} %get-tuple-element.25), channel_id=1, source_target_pairs={{0,4},{4,0},{8,12},{12,8},{16,20},{20,16},{24,28},{28,24},{1,5},{5... | collective-permute-start | bytes 1769480 | tf_op jit(solution)/shard_map/ppermute | solution.py:423
  20.5 3.4 %collective-permute-start.7 = (bf16[4,96,768]{2,1,0:T(8,128)(2,1)S(1)}, bf16[4,96,768]{2,1,0:T(8,128)(2,1)S(1)}, u32[]{:S(2)}, u32[]{:S(2)}) collective-permute-start(bf16[4,96,768]{2,1,0:T(8,128)(2,1)S(1)} %stack.1.refs_0_), channel_id=1, source_target_pairs={{0,4},{4,0},{8,12},{12,8},{16,20},{20,16},{24,28},{28,24},{1,5},{5... | collective-permute-start | bytes 1769480 | tf_op jit(solution)/shard_map/ppermute | solution.py:374
  22.5 9.1 %collective-permute-start.10 = (bf16[2,96,768]{2,1,0:T(8,128)(2,1)S(1)}, bf16[2,96,768]{2,1,0:T(8,128)(2,1)S(1)}, u32[]{:S(2)}, u32[]{:S(2)}) collective-permute-start(bf16[2,96,768]{2,1,0:T(8,128)(2,1)S(1)} %get-tuple-element.26), channel_id=1, source_target_pairs={{0,8},{4,12},{8,0},{12,4},{16,24},{20,28},{24,16},{28,20},{1,9},{5... | collective-permute-start | bytes 884744 | tf_op jit(solution)/shard_map/ppermute | solution.py:423
  27.1 12.1 %collective-permute-start.9 = (bf16[4,32,768]{2,1,0:T(8,128)(2,1)S(1)}, bf16[4,32,768]{2,1,0:T(8,128)(2,1)S(1)}, u32[]{:S(2)}, u32[]{:S(2)}) collective-permute-start(bf16[4,32,768]{2,1,0:T(8,128)(2,1)S(1)} %backward.5), channel_id=1, source_target_pairs={{0,3},{1,2},{2,1},{3,0},{4,7},{5,6},{6,5},{7,4},{8,11},{9,10},{10,... | collective-permute-start | bytes 589832 | tf_op jit(solution)/shard_map/ppermute | solution.py:381
  31.0 8.2 %collective-permute-start.8 = (bf16[4,32,768]{2,1,0:T(8,128)(2,1)S(1)}, bf16[4,32,768]{2,1,0:T(8,128)(2,1)S(1)}, u32[]{:S(2)}, u32[]{:S(2)}) collective-permute-start(bf16[4,32,768]{2,1,0:T(8,128)(2,1)S(1)} %backward.4), channel_id=1, source_target_pairs={{0,2},{1,3},{2,0},{3,1},{4,6},{5,7},{6,4},{7,5},{8,10},{9,11},{10,... | collective-permute-start | bytes 589832 | tf_op jit(solution)/shard_map/ppermute | solution.py:381
  31.7 9.8 %collective-permute-start.12 = (bf16[1,96,768]{2,1,0:T(8,128)(2,1)S(1)}, bf16[1,96,768]{2,1,0:T(8,128)(2,1)S(1)}, u32[]{:S(2)}, u32[]{:S(2)}) collective-permute-start(bf16[1,96,768]{2,1,0:T(8,128)(2,1)S(1)} %get-tuple-element.33), channel_id=1, source_target_pairs={{0,16},{4,20},{8,24},{12,28},{16,0},{20,4},{24,8},{28,12},{1,17},{... | collective-permute-start | bytes 442376 | tf_op jit(solution)/shard_map/ppermute | solution.py:423
  36.3 5.9 %collective-permute-start.11 = (bf16[4,32,768]{2,1,0:T(8,128)(2,1)S(1)}, bf16[4,32,768]{2,1,0:T(8,128)(2,1)S(1)}, u32[]{:S(2)}, u32[]{:S(2)}) collective-permute-start(bf16[4,32,768]{2,1,0:T(8,128)(2,1)S(1)} %backward.6), channel_id=1, source_target_pairs={{0,1},{1,0},{2,3},{3,2},{4,5},{5,4},{6,7},{7,6},{8,9},{9,8},{10,11... | collective-permute-start | bytes 589832 | tf_op jit(solution)/shard_map/ppermute | solution.py:381

commit v3 on v0

--- a/solution.py
+++ b/solution.py
@@ -340,20 +340,13 @@
     return run(functools.partial(fold_kernel, level), outs, (held, got), name="fold")
 
 
-def finish_kernel(count, parts, *refs):
-    back_refs, weight_refs, (back_ref, weight_ref) = refs[:parts], refs[parts:-2], refs[-2:]
-
-    def total(values):
-        return sum(ref[...].astype(jnp.float32) for ref in values)
-
-    back_ref[...] = total(back_refs).astype(back_ref.dtype)
-    weight_ref[...] = total(weight_refs) / count
-
-
-def finish(backs, weights, count):
-    outs = [bf16(*backs[0].shape), f32(*weights[0].shape)]
-    kernel = functools.partial(finish_kernel, count, len(backs))
-    return run(kernel, outs, (*backs, *weights), name="finish")
+def finish_kernel(count, *refs):
+    total = sum(ref[...].astype(jnp.float32) for ref in refs[:-1])
+    refs[-1][...] = (total / count if count > 1 else total).astype(refs[-1].dtype)
+
+
+def finish(out, parts, count=1):
+    return run(functools.partial(finish_kernel, count), [out], parts, name="finish")[0]
 
 
 def parity_and_place():
@@ -471,7 +464,9 @@
     for i in [*range(2, bands), 1, 0]:
         ready = sends[min(1, len(sends) - 1)] if i > 1 else sends[-1]
         backs.append(send_rows(backward(after(valid, ready), grad_mixed, wide, i, bands), i))
-    back, weight_grad = finish(backs, weights, count)
+    weight_grad = finish(f32(*weights[0].shape), weights, count)
+    backs[-2] = after(backs[-2], weight_grad)
+    back = finish(bf16(*backs[0].shape), backs)
     return (back[None], weight_grad)
 
 

time: 43.2 us -> 43.2 us (level)
  Pallas kernels: 15.9 us -> 16.6 us
  waiting for transfers between devices: 5.86 us -> 5.22 us
    ppermute x6, waiting for transfers between devices: 2.1 us -> 0.29 us  [send_rows(): lax.ppermute(value, 'rows', [(i, partner(i, index, count)) for i in range...]
    ppermute x3, waiting for transfers between devices: 2.06 us -> 3.23 us  [scatter_section(): got = lax.ppermute(send, 'section', way)]
    pallas_call x15 -> x16, Pallas kernels: 15.9 us -> 16.6 us  [run(): pl.pallas_call(kernel, out_shape=tuple(outs), in_specs=[smem if arg.dtype...]
  transfers between devices with their start and end apart: 13 -> 13, of which waited for: 8 -> 6; matrix products, arithmetic and copies ran while one was open for 0% -> 0% of each run, Pallas kernels for 35% -> 37%
where the time goes in v3:
time: 43.2 us; the launch traced here: 43 us
  starting transfers between devices  19.1 us (44%)
  Pallas kernels  16.6 us (38%)
  waiting for transfers between devices  5.22 us (12%)
  between operations  2.11 us (5%)
    pallas_call x16, Pallas kernels, run(): pl.pallas_call(kernel, out_shape=tuple(outs), in_specs=[smem if arg.dtype...  16.6 us
    ppermute x6, starting transfers between devices, send_rows(): lax.ppermute(value, 'rows', [(i, partner(i, index, count)) for i in range...  8.7 us
    ppermute x3, starting transfers between devices, send_section(): return lax.ppermute(value, 'section', way)  6.26 us
    ppermute x3, starting transfers between devices, scatter_section(): got = lax.ppermute(send, 'section', way)  4.04 us
    ppermute x3, waiting for transfers between devices, scatter_section(): got = lax.ppermute(send, 'section', way)  3.23 us
    ppermute x3, waiting for transfers between devices, send_section(): return lax.ppermute(value, 'section', way)  1.51 us
  transfers between devices with their start and end apart: 13, of which 6 were waited for; matrix products, arithmetic and copies ran while one was open for 0% of the time, Pallas kernels for 37%

profile of v3, /device:TPU:0, one launch (start us, length us, event | category | flops | bytes accessed | tf_op | source)
XLA Modules:
  0.0 43.0 jit_solution(337173475902621257)
XLA Ops:
  0.7 3.0 %collective-permute-start.3 = (bf16[4,32,768]{2,1,0:T(8,128)(2,1)}, bf16[4,32,768]{2,1,0:T(8,128)(2,1)S(1)}, u32[]{:S(2)}, u32[]{:S(2)}) collective-permute-start(bf16[4,32,768]{2,1,0:T(8,128)(2,1)} %bitcast.10), channel_id=1, source_target_pairs={{0,1},{1,0},{2,3},{3,2},{4,5},{5,4},{6,7},{7,6},{8,9},{9,8},{10,11... | collective-permute-start | bytes 589832 | tf_op jit(solution)/shard_map/ppermute | solution.py:374
  3.7 1.5 %collective-permute-start.1 = (bf16[4,32,768]{2,1,0:T(8,128)(2,1)}, bf16[4,32,768]{2,1,0:T(8,128)(2,1)S(1)}, u32[]{:S(2)}, u32[]{:S(2)}) collective-permute-start(bf16[4,32,768]{2,1,0:T(8,128)(2,1)} %bitcast.11), channel_id=1, source_target_pairs={{0,2},{1,3},{2,0},{3,1},{4,6},{5,7},{6,4},{7,5},{8,10},{9,11},{10,... | collective-permute-start | bytes 589832 | tf_op jit(solution)/shard_map/ppermute | solution.py:374
  5.2 2.0 %collective-permute-start = (bf16[96,768]{1,0:T(8,128)(2,1)}, bf16[96,768]{1,0:T(8,128)(2,1)S(1)}, u32[]{:S(2)}, u32[]{:S(2)}) collective-permute-start(bf16[96,768]{1,0:T(8,128)(2,1)} %refs_0_.1), channel_id=1, source_target_pairs={{0,8},{4,12},{8,0},{12,4},{16,24},{20,28},{24,16},{28,20},{1,9},{5... | collective-permute-start | bytes 442376 | tf_op jit(solution)/shard_map/ppermute | solution.py:380
  7.2 2.6 %collective-permute-start.5 = (bf16[96,768]{1,0:T(8,128)(2,1)}, bf16[96,768]{1,0:T(8,128)(2,1)S(1)}, u32[]{:S(2)}, u32[]{:S(2)}) collective-permute-start(bf16[96,768]{1,0:T(8,128)(2,1)} %refs_0_.1), channel_id=1, source_target_pairs={{0,16},{4,20},{8,24},{12,28},{16,0},{20,4},{24,8},{28,12},{1,17},{... | collective-permute-start | bytes 442376 | tf_op jit(solution)/shard_map/ppermute | solution.py:380
  11.4 2.7 %forward.2.refs_2_ = f32[6,22,32,128]{3,2,1,0:T(8,128)S(1)} custom-call(f32[16,32,128]{2,1,0:T(8,128)S(1)} %get-tuple-element.33.valid_ref, f32[49,8,768]{2,1,0:T(8,128)S(1)} %get-tuple-element.21.taps_ref, bf16[4,32,768]{2,1,0:T(8,128)(2,1)S(1)} %bitcast.14, bf16[4,32,768]{2,1,0:T(8,128)(2,1)S(1)} %collective-permute-done.3.refs_1_), custom_call_target="tpu_custom_call" | custom-call | flops 13872660480 | bytes 1 | tf_op jit(solution)/shard_map/forward/pallas_call | solution.py:29
  14.4 2.7 %forward.3.mixed = f32[6,22,32,128]{3,2,1,0:T(8,128)S(1)} custom-call(f32[16,32,128]{2,1,0:T(8,128)S(1)} %get-tuple-element.33.valid_ref, f32[49,8,768]{2,1,0:T(8,128)S(1)} %get-tuple-element.21.taps_ref, bf16[4,32,768]{2,1,0:T(8,128)(2,1)S(1)} %collective-permute-done.1.refs_0_, ...), custom_call_target="tpu_custom_call", output_to_operand_aliasing={{}: (4, {})} | custom-call | flops 1 | bytes 1 | tf_op jit(solution)/shard_map/forward/pallas_call | solution.py:29
  17.2 1.6 %collective-permute-start.6 = (bf16[96,768]{1,0:T(8,128)(2,1)S(1)}, bf16[96,768]{1,0:T(8,128)(2,1)S(1)}, u32[]{:S(2)}, u32[]{:S(2)}) collective-permute-start(bf16[96,768]{1,0:T(8,128)(2,1)S(1)} %collective-permute-done.5.refs_2_), channel_id=1, source_target_pairs={{0,8},{4,12},{8,0},{12,4},{16,24},{20,28},{24,16},{28,20},{1,9},{5... | collective-permute-start | bytes 442376 | tf_op jit(solution)/shard_map/ppermute | solution.py:380
  18.8 0.9 %normalise.1 = (bf16[512,768]{1,0:T(8,128)(2,1)S(1)}, f32[16,32,128]{2,1,0:T(8,128)S(1)}, f32[16,32,128]{2,1,0:T(8,128)S(1)}) custom-call(f32[16,32,128]{2,1,0:T(8,128)S(1)} %get-tuple-element.33.valid_ref, f32[6,22,32,128]{3,2,1,0:T(8,128)S(1)} %forward.3.mixed, f32[6,128]{1,0:T(8,128)S(1)} %bitcast.16, f32[6,128]{1,0:T(8,128)S(1)} %bitcast.18), custom_call_target="tpu_custom_call" | custom-call | flops 1 | bytes 1 | tf_op jit(solution)/shard_map/normalise/pallas_call | solution.py:29
  19.8 1.0 %outer.1 = (f32[8,96,768]{2,1,0:T(8,128)S(1)}, bf16[4,96,768]{2,1,0:T(8,128)(2,1)S(1)}) custom-call(bf16[512,768]{1,0:T(8,128)(2,1)S(1)} %get-tuple-element.22.normed_ref, bf16[512,768]{1,0:T(8,128)(2,1)S(1)} %bitcast.7), custom_call_target="tpu_custom_call" | custom-call | flops 1 | bytes 1 | tf_op jit(solution)/shard_map/outer/pallas_call | solution.py:29
  20.9 1.5 %collective-permute-done.6.refs_3_ = bf16[96,768]{1,0:T(8,128)(2,1)S(1)} collective-permute-done((bf16[96,768]{1,0:T(8,128)(2,1)S(1)}, bf16[96,768]{1,0:T(8,128)(2,1)S(1)}, u32[]{:S(2)}, u32[]{:S(2)}) %collective-permute-start.6) | collective-permute-done | bytes 147488 | tf_op jit(solution)/shard_map/ppermute | solution.py:380
  22.5 0.4 collective-permute-done.4.got_ref
  23.0 1.3 %collective-permute-start.10 = (bf16[2,96,768]{2,1,0:T(8,128)(2,1)S(1)}, bf16[2,96,768]{2,1,0:T(8,128)(2,1)S(1)}, u32[]{:S(2)}, u32[]{:S(2)}) collective-permute-start(bf16[2,96,768]{2,1,0:T(8,128)(2,1)S(1)} %get-tuple-element.25), channel_id=1, source_target_pairs={{0,8},{4,12},{8,0},{12,4},{16,24},{20,28},{24,16},{28,20},{1,9},{5... | collective-permute-start | bytes 884744 | tf_op jit(solution)/shard_map/ppermute | solution.py:416
  24.5 2.0 %project.1.grad_ref = f32[6,22,48,128]{3,2,1,0:T(8,128)S(1)} custom-call(f32[16,32,128]{2,1,0:T(8,128)S(1)} %get-tuple-element.33.valid_ref, bf16[512,768]{1,0:T(8,128)(2,1)S(1)} %bitcast.8, f32[6,22,32,128]{3,2,1,0:T(8,128)S(1)} %forward.3.mixed, f32[16,32,128]{2,1,0:T(8,128)S(1)} %get-tuple-element.28.centres, ...), custom_call_target="tpu_custom_call" | custom-call | flops 1557135360 | bytes 4325376 | tf_op jit(solution)/shard_map/project/pallas_call | solution.py:29
  26.5 1.3 %backward.5 = bf16[4,32,768]{2,1,0:T(8,128)(2,1)S(1)} custom-call(f32[16,32,128]{2,1,0:T(8,128)S(1)} %get-tuple-element.33.valid_ref, f32[6,22,48,128]{3,2,1,0:T(8,128)S(1)} %project.1.grad_ref, f32[49,8,768]{2,1,0:T(8,128)S(1)} %get-tuple-element.21.taps_ref), custom_call_target="tpu_custom_call" | custom-call | flops 2312110080 | bytes 1 | tf_op jit(solution)/shard_map/backward/pallas_call | solution.py:29
  27.8 2.3 %collective-permute-start.9 = (bf16[4,32,768]{2,1,0:T(8,128)(2,1)S(1)}, bf16[4,32,768]{2,1,0:T(8,128)(2,1)S(1)}, u32[]{:S(2)}, u32[]{:S(2)}) collective-permute-start(bf16[4,32,768]{2,1,0:T(8,128)(2,1)S(1)} %backward.5), channel_id=1, source_target_pairs={{0,3},{1,2},{2,1},{3,0},{4,7},{5,6},{6,5},{7,4},{8,11},{9,10},{10,... | collective-permute-start | bytes 589832 | tf_op jit(solution)/shard_map/ppermute | solution.py:374
  30.1 1.3 %backward.4 = bf16[4,32,768]{2,1,0:T(8,128)(2,1)S(1)} custom-call(f32[16,32,128]{2,1,0:T(8,128)S(1)} %get-tuple-element.33.valid_ref, f32[6,22,48,128]{3,2,1,0:T(8,128)S(1)} %project.1.grad_ref, f32[49,8,768]{2,1,0:T(8,128)S(1)} %get-tuple-element.21.taps_ref), custom_call_target="tpu_custom_call" | custom-call | flops 2312110080 | bytes 1 | tf_op jit(solution)/shard_map/backward/pallas_call | solution.py:29
  31.4 0.6 %collective-permute-start.8 = (bf16[4,32,768]{2,1,0:T(8,128)(2,1)S(1)}, bf16[4,32,768]{2,1,0:T(8,128)(2,1)S(1)}, u32[]{:S(2)}, u32[]{:S(2)}) collective-permute-start(bf16[4,32,768]{2,1,0:T(8,128)(2,1)S(1)} %backward.4), channel_id=1, source_target_pairs={{0,2},{1,3},{2,0},{3,1},{4,6},{5,7},{6,4},{7,5},{8,10},{9,11},{10,... | collective-permute-start | bytes 589832 | tf_op jit(solution)/shard_map/ppermute | solution.py:374
  32.2 2.7 %collective-permute-start.12 = (bf16[1,96,768]{2,1,0:T(8,128)(2,1)S(1)}, bf16[1,96,768]{2,1,0:T(8,128)(2,1)S(1)}, u32[]{:S(2)}, u32[]{:S(2)}) collective-permute-start(bf16[1,96,768]{2,1,0:T(8,128)(2,1)S(1)} %get-tuple-element.32), channel_id=1, source_target_pairs={{0,16},{4,20},{8,24},{12,28},{16,0},{20,4},{24,8},{28,12},{1,17},{... | collective-permute-start | bytes 442376 | tf_op jit(solution)/shard_map/ppermute | solution.py:416
  34.8 1.3 %backward.6 = bf16[4,32,768]{2,1,0:T(8,128)(2,1)S(1)} custom-call(f32[16,32,128]{2,1,0:T(8,128)S(1)} %get-tuple-element.33.valid_ref, f32[6,22,48,128]{3,2,1,0:T(8,128)S(1)} %project.1.grad_ref, f32[49,8,768]{2,1,0:T(8,128)S(1)} %get-tuple-element.21.taps_ref), custom_call_target="tpu_custom_call" | custom-call | flops 2312110080 | bytes 1 | tf_op jit(solution)/shard_map/backward/pallas_call | solution.py:29
  36.1 1.3 %collective-permute-start.11 = (bf16[4,32,768]{2,1,0:T(8,128)(2,1)S(1)}, bf16[4,32,768]{2,1,0:T(8,128)(2,1)S(1)}, u32[]{:S(2)}, u32[]{:S(2)}) collective-permute-start(bf16[4,32,768]{2,1,0:T(8,128)(2,1)S(1)} %backward.6), channel_id=1, source_target_pairs={{0,1},{1,0},{2,3},{3,2},{4,5},{5,4},{6,7},{7,6},{8,9},{9,8},{10,11... | collective-permute-start | bytes 589832 | tf_op jit(solution)/shard_map/ppermute | solution.py:374
  37.5 1.3 %backward.7.refs_3_ = f32[4,32,768]{2,1,0:T(8,128)S(1)} custom-call(f32[16,32,128]{2,1,0:T(8,128)S(1)} %get-tuple-element.33.valid_ref, f32[6,22,48,128]{3,2,1,0:T(8,128)S(1)} %project.1.grad_ref, f32[49,8,768]{2,1,0:T(8,128)S(1)} %get-tuple-element.21.taps_ref), custom_call_target="tpu_custom_call" | custom-call | flops 2312110080 | bytes 1 | tf_op jit(solution)/shard_map/backward/pallas_call | solution.py:29
  38.8 2.7 %collective-permute-done.12 = bf16[1,96,768]{2,1,0:T(8,128)(2,1)S(1)} collective-permute-done((bf16[1,96,768]{2,1,0:T(8,128)(2,1)S(1)}, bf16[1,96,768]{2,1,0:T(8,128)(2,1)S(1)}, u32[]{:S(2)}, u32[]{:S(2)}) %collective-permute-start.12) | collective-permute-done | bytes 147488 | tf_op jit(solution)/shard_map/ppermute | solution.py:416
  41.5 0.8 %finish.2 = f32[96,768]{1,0:T(8,128)} custom-call(f32[96,768]{1,0:T(8,128)S(1)} %bitcast.9, bf16[96,768]{1,0:T(8,128)(2,1)S(1)} %bitcast.15), custom_call_target="tpu_custom_call" | custom-call | flops 1 | bytes 1 | tf_op jit(solution)/shard_map/finish/pallas_call | solution.py:29
  42.2 0.8 %finish.3 = bf16[4,32,768]{2,1,0:T(8,128)(2,1)} custom-call(bf16[4,32,768]{2,1,0:T(8,128)(2,1)S(1)} %collective-permute-done.8.refs_0_, bf16[4,32,768]{2,1,0:T(8,128)(2,1)S(1)} %collective-permute-done.9.refs_1_, bf16[4,32,768]{2,1,0:T(8,128)(2,1)S(1)} %collective-permute-done.11.refs_2_, f32[4,32,768]{2,1,0:T(8,128)S(1)} %backward.7.refs_3_), custom_call_target="tpu_custom_call" | custom-call | flops 1 | bytes 1 | tf_op jit(solution)/shard_map/finish/pallas_call | solution.py:29
  (30 shorter events, 1.3 us)
Async XLA Ops:
  0.6 10.5 %copy-start.1 = (bf16[1,4,32,768]{3,2,1,0:T(8,128)(2,1)S(1)}, bf16[1,4,32,768]{3,2,1,0:T(8,128)(2,1)}, u32[]{:S(2)}) copy-start(bf16[1,4,32,768]{3,2,1,0:T(8,128)(2,1)} %param.8) | copy-start | bytes 589828
  0.6 10.5 %copy-start.3 = (bf16[49,768]{1,0:T(8,128)(2,1)S(1)}, bf16[49,768]{1,0:T(8,128)(2,1)}, u32[]{:S(2)}) copy-start(bf16[49,768]{1,0:T(8,128)(2,1)} %taps_ref.1) | copy-start | bytes 225796
  0.7 10.7 %collective-permute-start.3 = (bf16[4,32,768]{2,1,0:T(8,128)(2,1)}, bf16[4,32,768]{2,1,0:T(8,128)(2,1)S(1)}, u32[]{:S(2)}, u32[]{:S(2)}) collective-permute-start(bf16[4,32,768]{2,1,0:T(8,128)(2,1)} %bitcast.10), channel_id=1, source_target_pairs={{0,1},{1,0},{2,3},{3,2},{4,5},{5,4},{6,7},{7,6},{8,9},{9,8},{10,11... | collective-permute-start | bytes 589832 | tf_op jit(solution)/shard_map/ppermute | solution.py:374
  3.7 10.8 %collective-permute-start.1 = (bf16[4,32,768]{2,1,0:T(8,128)(2,1)}, bf16[4,32,768]{2,1,0:T(8,128)(2,1)S(1)}, u32[]{:S(2)}, u32[]{:S(2)}) collective-permute-start(bf16[4,32,768]{2,1,0:T(8,128)(2,1)} %bitcast.11), channel_id=1, source_target_pairs={{0,2},{1,3},{2,0},{3,1},{4,6},{5,7},{6,4},{7,5},{8,10},{9,11},{10,... | collective-permute-start | bytes 589832 | tf_op jit(solution)/shard_map/ppermute | solution.py:374
  5.2 9.3 %collective-permute-start.2 = (bf16[4,32,768]{2,1,0:T(8,128)(2,1)}, bf16[4,32,768]{2,1,0:T(8,128)(2,1)S(1)}, u32[]{:S(2)}, u32[]{:S(2)}) collective-permute-start(bf16[4,32,768]{2,1,0:T(8,128)(2,1)} %bitcast.12), channel_id=1, source_target_pairs={{0,3},{1,2},{2,1},{3,0},{4,7},{5,6},{6,5},{7,4},{8,11},{9,10},{10,... | collective-permute-start | bytes 589832 | tf_op jit(solution)/shard_map/ppermute | solution.py:374
  5.2 13.6 %collective-permute-start = (bf16[96,768]{1,0:T(8,128)(2,1)}, bf16[96,768]{1,0:T(8,128)(2,1)S(1)}, u32[]{:S(2)}, u32[]{:S(2)}) collective-permute-start(bf16[96,768]{1,0:T(8,128)(2,1)} %refs_0_.1), channel_id=1, source_target_pairs={{0,8},{4,12},{8,0},{12,4},{16,24},{20,28},{24,16},{28,20},{1,9},{5... | collective-permute-start | bytes 442376 | tf_op jit(solution)/shard_map/ppermute | solution.py:380
  7.2 9.9 %collective-permute-start.5 = (bf16[96,768]{1,0:T(8,128)(2,1)}, bf16[96,768]{1,0:T(8,128)(2,1)S(1)}, u32[]{:S(2)}, u32[]{:S(2)}) collective-permute-start(bf16[96,768]{1,0:T(8,128)(2,1)} %refs_0_.1), channel_id=1, source_target_pairs={{0,16},{4,20},{8,24},{12,28},{16,0},{20,4},{24,8},{28,12},{1,17},{... | collective-permute-start | bytes 442376 | tf_op jit(solution)/shard_map/ppermute | solution.py:380
  14.1 4.7 %copy-start.4 = (f32[768]{0:T(1024)S(1)}, f32[768]{0:T(1024)}, u32[]{:S(2)}) copy-start(f32[768]{0:T(1024)} %param.12) | copy-start | bytes 9220
  14.2 4.7 %copy-start.5 = (f32[768]{0:T(1024)S(1)}, f32[768]{0:T(1024)}, u32[]{:S(2)}) copy-start(f32[768]{0:T(1024)} %param.13) | copy-start | bytes 9220
  17.2 2.6 %copy-start = (bf16[1,16,32,768]{3,2,1,0:T(8,128)(2,1)S(1)}, bf16[1,16,32,768]{3,2,1,0:T(8,128)(2,1)}, u32[]{:S(2)}) copy-start(bf16[1,16,32,768]{3,2,1,0:T(8,128)(2,1)} %param.9) | copy-start | bytes 2359300
  17.2 5.2 %copy-start.2 = (bf16[96,768]{1,0:T(8,128)(2,1)S(1)}, bf16[96,768]{1,0:T(8,128)(2,1)}, u32[]{:S(2)}) copy-start(bf16[96,768]{1,0:T(8,128)(2,1)} %refs_0_.1) | copy-start | bytes 442372
  17.2 5.2 %collective-permute-start.6 = (bf16[96,768]{1,0:T(8,128)(2,1)S(1)}, bf16[96,768]{1,0:T(8,128)(2,1)S(1)}, u32[]{:S(2)}, u32[]{:S(2)}) collective-permute-start(bf16[96,768]{1,0:T(8,128)(2,1)S(1)} %collective-permute-done.5.refs_2_), channel_id=1, source_target_pairs={{0,8},{4,12},{8,0},{12,4},{16,24},{20,28},{24,16},{28,20},{1,9},{5... | collective-permute-start | bytes 442376 | tf_op jit(solution)/shard_map/ppermute | solution.py:380
  20.8 2.1 %collective-permute-start.4 = (bf16[4,96,768]{2,1,0:T(8,128)(2,1)S(1)}, bf16[4,96,768]{2,1,0:T(8,128)(2,1)S(1)}, u32[]{:S(2)}, u32[]{:S(2)}) collective-permute-start(bf16[4,96,768]{2,1,0:T(8,128)(2,1)S(1)} %get-tuple-element.24), channel_id=1, source_target_pairs={{0,4},{4,0},{8,12},{12,8},{16,20},{20,16},{24,28},{28,24},{1,5},{5... | collective-permute-start | bytes 1769480 | tf_op jit(solution)/shard_map/ppermute | solution.py:416
  22.4 2.1 %collective-permute-start.7 = (bf16[4,96,768]{2,1,0:T(8,128)(2,1)S(1)}, bf16[4,96,768]{2,1,0:T(8,128)(2,1)S(1)}, u32[]{:S(2)}, u32[]{:S(2)}) collective-permute-start(bf16[4,96,768]{2,1,0:T(8,128)(2,1)S(1)} %stack.1.refs_0_), channel_id=1, source_target_pairs={{0,4},{4,0},{8,12},{12,8},{16,20},{20,16},{24,28},{28,24},{1,5},{5... | collective-permute-start | bytes 1769480 | tf_op jit(solution)/shard_map/ppermute | solution.py:367
  23.0 9.1 %collective-permute-start.10 = (bf16[2,96,768]{2,1,0:T(8,128)(2,1)S(1)}, bf16[2,96,768]{2,1,0:T(8,128)(2,1)S(1)}, u32[]{:S(2)}, u32[]{:S(2)}) collective-permute-start(bf16[2,96,768]{2,1,0:T(8,128)(2,1)S(1)} %get-tuple-element.25), channel_id=1, source_target_pairs={{0,8},{4,12},{8,0},{12,4},{16,24},{20,28},{24,16},{28,20},{1,9},{5... | collective-permute-start | bytes 884744 | tf_op jit(solution)/shard_map/ppermute | solution.py:416
  27.8 14.4 %collective-permute-start.9 = (bf16[4,32,768]{2,1,0:T(8,128)(2,1)S(1)}, bf16[4,32,768]{2,1,0:T(8,128)(2,1)S(1)}, u32[]{:S(2)}, u32[]{:S(2)}) collective-permute-start(bf16[4,32,768]{2,1,0:T(8,128)(2,1)S(1)} %backward.5), channel_id=1, source_target_pairs={{0,3},{1,2},{2,1},{3,0},{4,7},{5,6},{6,5},{7,4},{8,11},{9,10},{10,... | collective-permute-start | bytes 589832 | tf_op jit(solution)/shard_map/ppermute | solution.py:374
  31.4 10.8 %collective-permute-start.8 = (bf16[4,32,768]{2,1,0:T(8,128)(2,1)S(1)}, bf16[4,32,768]{2,1,0:T(8,128)(2,1)S(1)}, u32[]{:S(2)}, u32[]{:S(2)}) collective-permute-start(bf16[4,32,768]{2,1,0:T(8,128)(2,1)S(1)} %backward.4), channel_id=1, source_target_pairs={{0,2},{1,3},{2,0},{3,1},{4,6},{5,7},{6,4},{7,5},{8,10},{9,11},{10,... | collective-permute-start | bytes 589832 | tf_op jit(solution)/shard_map/ppermute | solution.py:374
  32.2 9.3 %collective-permute-start.12 = (bf16[1,96,768]{2,1,0:T(8,128)(2,1)S(1)}, bf16[1,96,768]{2,1,0:T(8,128)(2,1)S(1)}, u32[]{:S(2)}, u32[]{:S(2)}) collective-permute-start(bf16[1,96,768]{2,1,0:T(8,128)(2,1)S(1)} %get-tuple-element.32), channel_id=1, source_target_pairs={{0,16},{4,20},{8,24},{12,28},{16,0},{20,4},{24,8},{28,12},{1,17},{... | collective-permute-start | bytes 442376 | tf_op jit(solution)/shard_map/ppermute | solution.py:416
  36.1 6.1 %collective-permute-start.11 = (bf16[4,32,768]{2,1,0:T(8,128)(2,1)S(1)}, bf16[4,32,768]{2,1,0:T(8,128)(2,1)S(1)}, u32[]{:S(2)}, u32[]{:S(2)}) collective-permute-start(bf16[4,32,768]{2,1,0:T(8,128)(2,1)S(1)} %backward.6), channel_id=1, source_target_pairs={{0,1},{1,0},{2,3},{3,2},{4,5},{5,4},{6,7},{7,6},{8,9},{9,8},{10,11... | collective-permute-start | bytes 589832 | tf_op jit(solution)/shard_map/ppermute | solution.py:374

commit v4 on v3

--- a/solution.py
+++ b/solution.py
@@ -461,7 +461,7 @@
     grads = after(grad, sends[min(1, len(sends) - 1)])
     grad_mixed = project(valid, grads, mixed, centres, spreads, gain, proj_mine, proj_other)
     backs = []
-    for i in [*range(2, bands), 1, 0]:
+    for i in [*range(bands - 1, 1, -1), 1, 0]:
         ready = sends[min(1, len(sends) - 1)] if i > 1 else sends[-1]
         backs.append(send_rows(backward(after(valid, ready), grad_mixed, wide, i, bands), i))
     weight_grad = finish(f32(*weights[0].shape), weights, count)

time: 43.2 us -> 43.2 us (level)
  no operation moved by 1% of the time
where the time goes in v4:
time: 43.2 us; the launch traced here: 43 us
  starting transfers between devices  19.1 us (44%)
  Pallas kernels  16.6 us (38%)
  waiting for transfers between devices  5.22 us (12%)
  between operations  2.11 us (5%)
    pallas_call x16, Pallas kernels, run(): pl.pallas_call(kernel, out_shape=tuple(outs), in_specs=[smem if arg.dtype...  16.6 us
    ppermute x6, starting transfers between devices, send_rows(): lax.ppermute(value, 'rows', [(i, partner(i, index, count)) for i in range...  8.7 us
    ppermute x3, starting transfers between devices, send_section(): return lax.ppermute(value, 'section', way)  6.26 us
    ppermute x3, starting transfers between devices, scatter_section(): got = lax.ppermute(send, 'section', way)  4.04 us
    ppermute x3, waiting for transfers between devices, scatter_section(): got = lax.ppermute(send, 'section', way)  3.23 us
    ppermute x3, waiting for transfers between devices, send_section(): return lax.ppermute(value, 'section', way)  1.51 us
  transfers between devices with their start and end apart: 13, of which 6 were waited for; matrix products, arithmetic and copies ran while one was open for 0% of the time, Pallas kernels for 37%

profile of v4, /device:TPU:0, one launch (start us, length us, event | category | flops | bytes accessed | tf_op | source)
XLA Modules:
  0.0 43.0 jit_solution(2418292228804985056)
XLA Ops:
  0.7 3.0 %collective-permute-start.3 = (bf16[4,32,768]{2,1,0:T(8,128)(2,1)}, bf16[4,32,768]{2,1,0:T(8,128)(2,1)S(1)}, u32[]{:S(2)}, u32[]{:S(2)}) collective-permute-start(bf16[4,32,768]{2,1,0:T(8,128)(2,1)} %bitcast.10), channel_id=1, source_target_pairs={{0,1},{1,0},{2,3},{3,2},{4,5},{5,4},{6,7},{7,6},{8,9},{9,8},{10,11... | collective-permute-start | bytes 589832 | tf_op jit(solution)/shard_map/ppermute | solution.py:374
  3.7 1.5 %collective-permute-start.1 = (bf16[4,32,768]{2,1,0:T(8,128)(2,1)}, bf16[4,32,768]{2,1,0:T(8,128)(2,1)S(1)}, u32[]{:S(2)}, u32[]{:S(2)}) collective-permute-start(bf16[4,32,768]{2,1,0:T(8,128)(2,1)} %bitcast.11), channel_id=1, source_target_pairs={{0,2},{1,3},{2,0},{3,1},{4,6},{5,7},{6,4},{7,5},{8,10},{9,11},{10,... | collective-permute-start | bytes 589832 | tf_op jit(solution)/shard_map/ppermute | solution.py:374
  5.2 2.0 %collective-permute-start = (bf16[96,768]{1,0:T(8,128)(2,1)}, bf16[96,768]{1,0:T(8,128)(2,1)S(1)}, u32[]{:S(2)}, u32[]{:S(2)}) collective-permute-start(bf16[96,768]{1,0:T(8,128)(2,1)} %refs_0_.1), channel_id=1, source_target_pairs={{0,8},{4,12},{8,0},{12,4},{16,24},{20,28},{24,16},{28,20},{1,9},{5... | collective-permute-start | bytes 442376 | tf_op jit(solution)/shard_map/ppermute | solution.py:380
  7.2 2.6 %collective-permute-start.5 = (bf16[96,768]{1,0:T(8,128)(2,1)}, bf16[96,768]{1,0:T(8,128)(2,1)S(1)}, u32[]{:S(2)}, u32[]{:S(2)}) collective-permute-start(bf16[96,768]{1,0:T(8,128)(2,1)} %refs_0_.1), channel_id=1, source_target_pairs={{0,16},{4,20},{8,24},{12,28},{16,0},{20,4},{24,8},{28,12},{1,17},{... | collective-permute-start | bytes 442376 | tf_op jit(solution)/shard_map/ppermute | solution.py:380
  11.4 2.7 %forward.2.refs_2_ = f32[6,22,32,128]{3,2,1,0:T(8,128)S(1)} custom-call(f32[16,32,128]{2,1,0:T(8,128)S(1)} %get-tuple-element.33.valid_ref, f32[49,8,768]{2,1,0:T(8,128)S(1)} %get-tuple-element.21.taps_ref, bf16[4,32,768]{2,1,0:T(8,128)(2,1)S(1)} %bitcast.14, bf16[4,32,768]{2,1,0:T(8,128)(2,1)S(1)} %collective-permute-done.3.refs_1_), custom_call_target="tpu_custom_call" | custom-call | flops 13872660480 | bytes 1 | tf_op jit(solution)/shard_map/forward/pallas_call | solution.py:29
  14.4 2.7 %forward.3.mixed = f32[6,22,32,128]{3,2,1,0:T(8,128)S(1)} custom-call(f32[16,32,128]{2,1,0:T(8,128)S(1)} %get-tuple-element.33.valid_ref, f32[49,8,768]{2,1,0:T(8,128)S(1)} %get-tuple-element.21.taps_ref, bf16[4,32,768]{2,1,0:T(8,128)(2,1)S(1)} %collective-permute-done.1.refs_0_, ...), custom_call_target="tpu_custom_call", output_to_operand_aliasing={{}: (4, {})} | custom-call | flops 1 | bytes 1 | tf_op jit(solution)/shard_map/forward/pallas_call | solution.py:29
  17.2 1.6 %collective-permute-start.6 = (bf16[96,768]{1,0:T(8,128)(2,1)S(1)}, bf16[96,768]{1,0:T(8,128)(2,1)S(1)}, u32[]{:S(2)}, u32[]{:S(2)}) collective-permute-start(bf16[96,768]{1,0:T(8,128)(2,1)S(1)} %collective-permute-done.5.refs_2_), channel_id=1, source_target_pairs={{0,8},{4,12},{8,0},{12,4},{16,24},{20,28},{24,16},{28,20},{1,9},{5... | collective-permute-start | bytes 442376 | tf_op jit(solution)/shard_map/ppermute | solution.py:380
  18.8 0.9 %normalise.1 = (bf16[512,768]{1,0:T(8,128)(2,1)S(1)}, f32[16,32,128]{2,1,0:T(8,128)S(1)}, f32[16,32,128]{2,1,0:T(8,128)S(1)}) custom-call(f32[16,32,128]{2,1,0:T(8,128)S(1)} %get-tuple-element.33.valid_ref, f32[6,22,32,128]{3,2,1,0:T(8,128)S(1)} %forward.3.mixed, f32[6,128]{1,0:T(8,128)S(1)} %bitcast.16, f32[6,128]{1,0:T(8,128)S(1)} %bitcast.18), custom_call_target="tpu_custom_call" | custom-call | flops 1 | bytes 1 | tf_op jit(solution)/shard_map/normalise/pallas_call | solution.py:29
  19.8 1.0 %outer.1 = (f32[8,96,768]{2,1,0:T(8,128)S(1)}, bf16[4,96,768]{2,1,0:T(8,128)(2,1)S(1)}) custom-call(bf16[512,768]{1,0:T(8,128)(2,1)S(1)} %get-tuple-element.22.normed_ref, bf16[512,768]{1,0:T(8,128)(2,1)S(1)} %bitcast.7), custom_call_target="tpu_custom_call" | custom-call | flops 1 | bytes 1 | tf_op jit(solution)/shard_map/outer/pallas_call | solution.py:29
  20.9 1.5 %collective-permute-done.6.refs_3_ = bf16[96,768]{1,0:T(8,128)(2,1)S(1)} collective-permute-done((bf16[96,768]{1,0:T(8,128)(2,1)S(1)}, bf16[96,768]{1,0:T(8,128)(2,1)S(1)}, u32[]{:S(2)}, u32[]{:S(2)}) %collective-permute-start.6) | collective-permute-done | bytes 147488 | tf_op jit(solution)/shard_map/ppermute | solution.py:380
  22.5 0.4 collective-permute-done.4.got_ref
  23.0 1.3 %collective-permute-start.10 = (bf16[2,96,768]{2,1,0:T(8,128)(2,1)S(1)}, bf16[2,96,768]{2,1,0:T(8,128)(2,1)S(1)}, u32[]{:S(2)}, u32[]{:S(2)}) collective-permute-start(bf16[2,96,768]{2,1,0:T(8,128)(2,1)S(1)} %get-tuple-element.25), channel_id=1, source_target_pairs={{0,8},{4,12},{8,0},{12,4},{16,24},{20,28},{24,16},{28,20},{1,9},{5... | collective-permute-start | bytes 884744 | tf_op jit(solution)/shard_map/ppermute | solution.py:416
  24.5 2.0 %project.1.grad_ref = f32[6,22,48,128]{3,2,1,0:T(8,128)S(1)} custom-call(f32[16,32,128]{2,1,0:T(8,128)S(1)} %get-tuple-element.33.valid_ref, bf16[512,768]{1,0:T(8,128)(2,1)S(1)} %bitcast.8, f32[6,22,32,128]{3,2,1,0:T(8,128)S(1)} %forward.3.mixed, f32[16,32,128]{2,1,0:T(8,128)S(1)} %get-tuple-element.28.centres, ...), custom_call_target="tpu_custom_call" | custom-call | flops 1557135360 | bytes 4325376 | tf_op jit(solution)/shard_map/project/pallas_call | solution.py:29
  26.5 1.3 %backward.5 = bf16[4,32,768]{2,1,0:T(8,128)(2,1)S(1)} custom-call(f32[16,32,128]{2,1,0:T(8,128)S(1)} %get-tuple-element.33.valid_ref, f32[6,22,48,128]{3,2,1,0:T(8,128)S(1)} %project.1.grad_ref, f32[49,8,768]{2,1,0:T(8,128)S(1)} %get-tuple-element.21.taps_ref), custom_call_target="tpu_custom_call" | custom-call | flops 2312110080 | bytes 1 | tf_op jit(solution)/shard_map/backward/pallas_call | solution.py:29
  27.8 1.6 %collective-permute-start.9 = (bf16[4,32,768]{2,1,0:T(8,128)(2,1)S(1)}, bf16[4,32,768]{2,1,0:T(8,128)(2,1)S(1)}, u32[]{:S(2)}, u32[]{:S(2)}) collective-permute-start(bf16[4,32,768]{2,1,0:T(8,128)(2,1)S(1)} %backward.5), channel_id=1, source_target_pairs={{0,2},{1,3},{2,0},{3,1},{4,6},{5,7},{6,4},{7,5},{8,10},{9,11},{10,... | collective-permute-start | bytes 589832 | tf_op jit(solution)/shard_map/ppermute | solution.py:374
  29.4 1.3 %backward.4 = bf16[4,32,768]{2,1,0:T(8,128)(2,1)S(1)} custom-call(f32[16,32,128]{2,1,0:T(8,128)S(1)} %get-tuple-element.33.valid_ref, f32[6,22,48,128]{3,2,1,0:T(8,128)S(1)} %project.1.grad_ref, f32[49,8,768]{2,1,0:T(8,128)S(1)} %get-tuple-element.21.taps_ref), custom_call_target="tpu_custom_call" | custom-call | flops 2312110080 | bytes 1 | tf_op jit(solution)/shard_map/backward/pallas_call | solution.py:29
  30.7 1.3 %collective-permute-start.8 = (bf16[4,32,768]{2,1,0:T(8,128)(2,1)S(1)}, bf16[4,32,768]{2,1,0:T(8,128)(2,1)S(1)}, u32[]{:S(2)}, u32[]{:S(2)}) collective-permute-start(bf16[4,32,768]{2,1,0:T(8,128)(2,1)S(1)} %backward.4), channel_id=1, source_target_pairs={{0,3},{1,2},{2,1},{3,0},{4,7},{5,6},{6,5},{7,4},{8,11},{9,10},{10,... | collective-permute-start | bytes 589832 | tf_op jit(solution)/shard_map/ppermute | solution.py:374
  32.2 2.7 %collective-permute-start.12 = (bf16[1,96,768]{2,1,0:T(8,128)(2,1)S(1)}, bf16[1,96,768]{2,1,0:T(8,128)(2,1)S(1)}, u32[]{:S(2)}, u32[]{:S(2)}) collective-permute-start(bf16[1,96,768]{2,1,0:T(8,128)(2,1)S(1)} %get-tuple-element.32), channel_id=1, source_target_pairs={{0,16},{4,20},{8,24},{12,28},{16,0},{20,4},{24,8},{28,12},{1,17},{... | collective-permute-start | bytes 442376 | tf_op jit(solution)/shard_map/ppermute | solution.py:416
  34.8 1.3 %backward.6 = bf16[4,32,768]{2,1,0:T(8,128)(2,1)S(1)} custom-call(f32[16,32,128]{2,1,0:T(8,128)S(1)} %get-tuple-element.33.valid_ref, f32[6,22,48,128]{3,2,1,0:T(8,128)S(1)} %project.1.grad_ref, f32[49,8,768]{2,1,0:T(8,128)S(1)} %get-tuple-element.21.taps_ref), custom_call_target="tpu_custom_call" | custom-call | flops 2312110080 | bytes 1 | tf_op jit(solution)/shard_map/backward/pallas_call | solution.py:29
  36.1 1.3 %collective-permute-start.11 = (bf16[4,32,768]{2,1,0:T(8,128)(2,1)S(1)}, bf16[4,32,768]{2,1,0:T(8,128)(2,1)S(1)}, u32[]{:S(2)}, u32[]{:S(2)}) collective-permute-start(bf16[4,32,768]{2,1,0:T(8,128)(2,1)S(1)} %backward.6), channel_id=1, source_target_pairs={{0,1},{1,0},{2,3},{3,2},{4,5},{5,4},{6,7},{7,6},{8,9},{9,8},{10,11... | collective-permute-start | bytes 589832 | tf_op jit(solution)/shard_map/ppermute | solution.py:374
  37.5 1.3 %backward.7.refs_3_ = f32[4,32,768]{2,1,0:T(8,128)S(1)} custom-call(f32[16,32,128]{2,1,0:T(8,128)S(1)} %get-tuple-element.33.valid_ref, f32[6,22,48,128]{3,2,1,0:T(8,128)S(1)} %project.1.grad_ref, f32[49,8,768]{2,1,0:T(8,128)S(1)} %get-tuple-element.21.taps_ref), custom_call_target="tpu_custom_call" | custom-call | flops 2312110080 | bytes 1 | tf_op jit(solution)/shard_map/backward/pallas_call | solution.py:29
  38.8 2.7 %collective-permute-done.12 = bf16[1,96,768]{2,1,0:T(8,128)(2,1)S(1)} collective-permute-done((bf16[1,96,768]{2,1,0:T(8,128)(2,1)S(1)}, bf16[1,96,768]{2,1,0:T(8,128)(2,1)S(1)}, u32[]{:S(2)}, u32[]{:S(2)}) %collective-permute-start.12) | collective-permute-done | bytes 147488 | tf_op jit(solution)/shard_map/ppermute | solution.py:416
  41.5 0.8 %finish.2 = f32[96,768]{1,0:T(8,128)} custom-call(f32[96,768]{1,0:T(8,128)S(1)} %bitcast.9, bf16[96,768]{1,0:T(8,128)(2,1)S(1)} %bitcast.15), custom_call_target="tpu_custom_call" | custom-call | flops 1 | bytes 1 | tf_op jit(solution)/shard_map/finish/pallas_call | solution.py:29
  42.2 0.8 %finish.3 = bf16[4,32,768]{2,1,0:T(8,128)(2,1)} custom-call(bf16[4,32,768]{2,1,0:T(8,128)(2,1)S(1)} %collective-permute-done.8.refs_0_, bf16[4,32,768]{2,1,0:T(8,128)(2,1)S(1)} %collective-permute-done.9.refs_1_, bf16[4,32,768]{2,1,0:T(8,128)(2,1)S(1)} %collective-permute-done.11.refs_2_, f32[4,32,768]{2,1,0:T(8,128)S(1)} %backward.7.refs_3_), custom_call_target="tpu_custom_call" | custom-call | flops 1 | bytes 1 | tf_op jit(solution)/shard_map/finish/pallas_call | solution.py:29
  (30 shorter events, 1.3 us)
Async XLA Ops:
  0.6 10.5 %copy-start.1 = (bf16[1,4,32,768]{3,2,1,0:T(8,128)(2,1)S(1)}, bf16[1,4,32,768]{3,2,1,0:T(8,128)(2,1)}, u32[]{:S(2)}) copy-start(bf16[1,4,32,768]{3,2,1,0:T(8,128)(2,1)} %param.8) | copy-start | bytes 589828
  0.6 10.5 %copy-start.3 = (bf16[49,768]{1,0:T(8,128)(2,1)S(1)}, bf16[49,768]{1,0:T(8,128)(2,1)}, u32[]{:S(2)}) copy-start(bf16[49,768]{1,0:T(8,128)(2,1)} %taps_ref.1) | copy-start | bytes 225796
  0.7 10.7 %collective-permute-start.3 = (bf16[4,32,768]{2,1,0:T(8,128)(2,1)}, bf16[4,32,768]{2,1,0:T(8,128)(2,1)S(1)}, u32[]{:S(2)}, u32[]{:S(2)}) collective-permute-start(bf16[4,32,768]{2,1,0:T(8,128)(2,1)} %bitcast.10), channel_id=1, source_target_pairs={{0,1},{1,0},{2,3},{3,2},{4,5},{5,4},{6,7},{7,6},{8,9},{9,8},{10,11... | collective-permute-start | bytes 589832 | tf_op jit(solution)/shard_map/ppermute | solution.py:374
  3.7 10.8 %collective-permute-start.1 = (bf16[4,32,768]{2,1,0:T(8,128)(2,1)}, bf16[4,32,768]{2,1,0:T(8,128)(2,1)S(1)}, u32[]{:S(2)}, u32[]{:S(2)}) collective-permute-start(bf16[4,32,768]{2,1,0:T(8,128)(2,1)} %bitcast.11), channel_id=1, source_target_pairs={{0,2},{1,3},{2,0},{3,1},{4,6},{5,7},{6,4},{7,5},{8,10},{9,11},{10,... | collective-permute-start | bytes 589832 | tf_op jit(solution)/shard_map/ppermute | solution.py:374
  5.2 9.3 %collective-permute-start.2 = (bf16[4,32,768]{2,1,0:T(8,128)(2,1)}, bf16[4,32,768]{2,1,0:T(8,128)(2,1)S(1)}, u32[]{:S(2)}, u32[]{:S(2)}) collective-permute-start(bf16[4,32,768]{2,1,0:T(8,128)(2,1)} %bitcast.12), channel_id=1, source_target_pairs={{0,3},{1,2},{2,1},{3,0},{4,7},{5,6},{6,5},{7,4},{8,11},{9,10},{10,... | collective-permute-start | bytes 589832 | tf_op jit(solution)/shard_map/ppermute | solution.py:374
  5.2 13.6 %collective-permute-start = (bf16[96,768]{1,0:T(8,128)(2,1)}, bf16[96,768]{1,0:T(8,128)(2,1)S(1)}, u32[]{:S(2)}, u32[]{:S(2)}) collective-permute-start(bf16[96,768]{1,0:T(8,128)(2,1)} %refs_0_.1), channel_id=1, source_target_pairs={{0,8},{4,12},{8,0},{12,4},{16,24},{20,28},{24,16},{28,20},{1,9},{5... | collective-permute-start | bytes 442376 | tf_op jit(solution)/shard_map/ppermute | solution.py:380
  7.2 9.9 %collective-permute-start.5 = (bf16[96,768]{1,0:T(8,128)(2,1)}, bf16[96,768]{1,0:T(8,128)(2,1)S(1)}, u32[]{:S(2)}, u32[]{:S(2)}) collective-permute-start(bf16[96,768]{1,0:T(8,128)(2,1)} %refs_0_.1), channel_id=1, source_target_pairs={{0,16},{4,20},{8,24},{12,28},{16,0},{20,4},{24,8},{28,12},{1,17},{... | collective-permute-start | bytes 442376 | tf_op jit(solution)/shard_map/ppermute | solution.py:380
  14.1 4.7 %copy-start.4 = (f32[768]{0:T(1024)S(1)}, f32[768]{0:T(1024)}, u32[]{:S(2)}) copy-start(f32[768]{0:T(1024)} %param.12) | copy-start | bytes 9220
  14.2 4.7 %copy-start.5 = (f32[768]{0:T(1024)S(1)}, f32[768]{0:T(1024)}, u32[]{:S(2)}) copy-start(f32[768]{0:T(1024)} %param.13) | copy-start | bytes 9220
  17.2 2.6 %copy-start = (bf16[1,16,32,768]{3,2,1,0:T(8,128)(2,1)S(1)}, bf16[1,16,32,768]{3,2,1,0:T(8,128)(2,1)}, u32[]{:S(2)}) copy-start(bf16[1,16,32,768]{3,2,1,0:T(8,128)(2,1)} %param.9) | copy-start | bytes 2359300
  17.2 5.2 %copy-start.2 = (bf16[96,768]{1,0:T(8,128)(2,1)S(1)}, bf16[96,768]{1,0:T(8,128)(2,1)}, u32[]{:S(2)}) copy-start(bf16[96,768]{1,0:T(8,128)(2,1)} %refs_0_.1) | copy-start | bytes 442372
  17.2 5.2 %collective-permute-start.6 = (bf16[96,768]{1,0:T(8,128)(2,1)S(1)}, bf16[96,768]{1,0:T(8,128)(2,1)S(1)}, u32[]{:S(2)}, u32[]{:S(2)}) collective-permute-start(bf16[96,768]{1,0:T(8,128)(2,1)S(1)} %collective-permute-done.5.refs_2_), channel_id=1, source_target_pairs={{0,8},{4,12},{8,0},{12,4},{16,24},{20,28},{24,16},{28,20},{1,9},{5... | collective-permute-start | bytes 442376 | tf_op jit(solution)/shard_map/ppermute | solution.py:380
  20.8 2.1 %collective-permute-start.4 = (bf16[4,96,768]{2,1,0:T(8,128)(2,1)S(1)}, bf16[4,96,768]{2,1,0:T(8,128)(2,1)S(1)}, u32[]{:S(2)}, u32[]{:S(2)}) collective-permute-start(bf16[4,96,768]{2,1,0:T(8,128)(2,1)S(1)} %get-tuple-element.24), channel_id=1, source_target_pairs={{0,4},{4,0},{8,12},{12,8},{16,20},{20,16},{24,28},{28,24},{1,5},{5... | collective-permute-start | bytes 1769480 | tf_op jit(solution)/shard_map/ppermute | solution.py:416
  22.4 2.1 %collective-permute-start.7 = (bf16[4,96,768]{2,1,0:T(8,128)(2,1)S(1)}, bf16[4,96,768]{2,1,0:T(8,128)(2,1)S(1)}, u32[]{:S(2)}, u32[]{:S(2)}) collective-permute-start(bf16[4,96,768]{2,1,0:T(8,128)(2,1)S(1)} %stack.1.refs_0_), channel_id=1, source_target_pairs={{0,4},{4,0},{8,12},{12,8},{16,20},{20,16},{24,28},{28,24},{1,5},{5... | collective-permute-start | bytes 1769480 | tf_op jit(solution)/shard_map/ppermute | solution.py:367
  23.0 9.1 %collective-permute-start.10 = (bf16[2,96,768]{2,1,0:T(8,128)(2,1)S(1)}, bf16[2,96,768]{2,1,0:T(8,128)(2,1)S(1)}, u32[]{:S(2)}, u32[]{:S(2)}) collective-permute-start(bf16[2,96,768]{2,1,0:T(8,128)(2,1)S(1)} %get-tuple-element.25), channel_id=1, source_target_pairs={{0,8},{4,12},{8,0},{12,4},{16,24},{20,28},{24,16},{28,20},{1,9},{5... | collective-permute-start | bytes 884744 | tf_op jit(solution)/shard_map/ppermute | solution.py:416
  27.8 14.4 %collective-permute-start.9 = (bf16[4,32,768]{2,1,0:T(8,128)(2,1)S(1)}, bf16[4,32,768]{2,1,0:T(8,128)(2,1)S(1)}, u32[]{:S(2)}, u32[]{:S(2)}) collective-permute-start(bf16[4,32,768]{2,1,0:T(8,128)(2,1)S(1)} %backward.5), channel_id=1, source_target_pairs={{0,2},{1,3},{2,0},{3,1},{4,6},{5,7},{6,4},{7,5},{8,10},{9,11},{10,... | collective-permute-start | bytes 589832 | tf_op jit(solution)/shard_map/ppermute | solution.py:374
  30.7 11.5 %collective-permute-start.8 = (bf16[4,32,768]{2,1,0:T(8,128)(2,1)S(1)}, bf16[4,32,768]{2,1,0:T(8,128)(2,1)S(1)}, u32[]{:S(2)}, u32[]{:S(2)}) collective-permute-start(bf16[4,32,768]{2,1,0:T(8,128)(2,1)S(1)} %backward.4), channel_id=1, source_target_pairs={{0,3},{1,2},{2,1},{3,0},{4,7},{5,6},{6,5},{7,4},{8,11},{9,10},{10,... | collective-permute-start | bytes 589832 | tf_op jit(solution)/shard_map/ppermute | solution.py:374
  32.2 9.3 %collective-permute-start.12 = (bf16[1,96,768]{2,1,0:T(8,128)(2,1)S(1)}, bf16[1,96,768]{2,1,0:T(8,128)(2,1)S(1)}, u32[]{:S(2)}, u32[]{:S(2)}) collective-permute-start(bf16[1,96,768]{2,1,0:T(8,128)(2,1)S(1)} %get-tuple-element.32), channel_id=1, source_target_pairs={{0,16},{4,20},{8,24},{12,28},{16,0},{20,4},{24,8},{28,12},{1,17},{... | collective-permute-start | bytes 442376 | tf_op jit(solution)/shard_map/ppermute | solution.py:416
  36.1 6.1 %collective-permute-start.11 = (bf16[4,32,768]{2,1,0:T(8,128)(2,1)S(1)}, bf16[4,32,768]{2,1,0:T(8,128)(2,1)S(1)}, u32[]{:S(2)}, u32[]{:S(2)}) collective-permute-start(bf16[4,32,768]{2,1,0:T(8,128)(2,1)S(1)} %backward.6), channel_id=1, source_target_pairs={{0,1},{1,0},{2,3},{3,2},{4,5},{5,4},{6,7},{7,6},{8,9},{9,8},{10,11... | collective-permute-start | bytes 589832 | tf_op jit(solution)/shard_map/ppermute | solution.py:374
